TPU v7x, 32 devices: a whole 2x2x4 slice. The times are simulated.
32 devices in a mesh: ctx: 8 (over y, x, core), tp: 4 (over z).
Axes of the slice: x: 2, y: 2, z: 4, core: 2. Of those that a mesh axis runs over, the one named last changes fastest.
Arguments:
- value_path: bfloat16 [1024, 8192], P('ctx', 'tp'), may hold values from -6 to 6
- key_se: bfloat16 [1024, 8192], P('ctx', 'tp'), may hold values from -6 to 6
- query_se: bfloat16 [1024, 8192], P('ctx', 'tp'), may hold values from -60 to 60
- key_mr: bfloat16 [1024, 8192], P('ctx', 'tp'), may hold values from -6 to 6
- query_mr: bfloat16 [1024, 8192], P('ctx', 'tp'), may hold values from -6 to 6
- out_grad: bfloat16 [1024, 8192], P('ctx', 'tp'), may hold values from -6 to 6
- norm_gain: bfloat16 [8192], P('tp'), may hold values from 0.099609375 to 1.8984375
- filter_se: bfloat16 [7, 8192], P(None, 'tp'), may hold values from -2 to 2
- filter_mr: bfloat16 [128, 8192], P(None, 'tp'), may hold values from -0.5 to 0.5
Outputs:
- grad_value: bfloat16 [1024, 8192], P('ctx', 'tp')
- grad_query_se: bfloat16 [1024, 8192], P('ctx', 'tp')
- grad_key_se: bfloat16 [1024, 8192], P('ctx', 'tp')
- grad_query_mr: bfloat16 [1024, 8192], P('ctx', 'tp')
- grad_key_mr: bfloat16 [1024, 8192], P('ctx', 'tp')
- grad_filter_se: float32 [7, 8192], P(None, 'tp')
- grad_filter_mr: float32 [128, 8192], P(None, 'tp')
- grad_gain: float32 [8192], P('tp')
All inputs are finite; a program needn't handle non-finite values.
Results may differ from a plain program's by a relative error of at most 0.015.
Values may be sent and summed in bfloat16 or wider, within the bound.
A program may use at most 64 MiB of HBM per device.

v0:
```python
import jax
import jax.numpy as jnp
from jax import lax
from jax.sharding import PartitionSpec as P

D = 8192


def shifted(block, axis, distance):
    devices = range(lax.axis_size(axis))
    route = [(i - distance, i) for i in devices if i - distance in devices]
    return lax.ppermute(block, axis, route)


def depthwise(lhs, kernel):
    out = lax.conv_general_dilated(
        lhs[None],
        kernel[:, None, :],
        (1,),
        "VALID",
        dimension_numbers=("NWC", "WIO", "NWC"),
        feature_group_count=lhs.shape[1],
        preferred_element_type=jnp.float32,
    )
    return out[0]


def from_left(block, width):
    return shifted(block[block.shape[0] - width :], "ctx", 1)


def from_right(block, width):
    return shifted(block[:width], "ctx", -1)


def token_total(partial_sum):
    return lax.psum(partial_sum, "tp")


def shards(
    value_path, key_se, query_se, key_mr, query_mr, out_grad, norm_gain, filter_se, filter_mr
):
    f32 = jnp.float32
    bf16 = jnp.bfloat16
    se_taps = filter_se.shape[0]
    mr_taps = filter_mr.shape[0]
    prod_se = (key_se.astype(f32) * value_path.astype(f32)).astype(bf16)
    grad_conv_mr = (out_grad.astype(f32) * query_mr.astype(f32)).astype(bf16)
    rim_se = from_left(prod_se, se_taps - 1)
    rim_grad_mr = from_right(grad_conv_mr, mr_taps - 1)
    pad_se = jnp.concatenate([rim_se, prod_se], axis=0)
    conv_se = depthwise(pad_se, filter_se[::-1])
    mixed_se = query_se.astype(f32) * conv_se
    grad_prod_mr = depthwise(jnp.concatenate([grad_conv_mr, rim_grad_mr], axis=0), filter_mr)
    gain = norm_gain.astype(f32)
    grad_normed = grad_prod_mr * key_mr.astype(f32)
    scaled = grad_normed * gain
    square_part = jnp.sum(mixed_se * mixed_se, axis=1, keepdims=True)
    dot_part = jnp.sum(scaled * mixed_se, axis=1, keepdims=True)
    square_total = token_total(square_part)
    inv_rms = lax.rsqrt(square_total / D + 1e-06)
    normed = (mixed_se * inv_rms * gain).astype(bf16)
    prod_mr = (key_mr.astype(f32) * normed.astype(f32)).astype(bf16)
    rim_mr = from_left(prod_mr, mr_taps - 1)
    pad_mr = jnp.concatenate([rim_mr, prod_mr], axis=0)
    conv_mr = depthwise(pad_mr, filter_mr[::-1])
    grad_query_mr = (out_grad.astype(f32) * conv_mr).astype(bf16)
    grad_key_mr = (grad_prod_mr * normed.astype(f32)).astype(bf16)
    local_filter_mr = depthwise(pad_mr, grad_conv_mr)[::-1]
    grad_filter_mr = lax.psum(local_filter_mr, "ctx")
    local_gain = jnp.sum(grad_normed * mixed_se * inv_rms, axis=0)
    dot_sum = token_total(dot_part)
    grad_mixed = inv_rms * scaled - mixed_se * (inv_rms * inv_rms * inv_rms) * dot_sum / D
    grad_query_se = (grad_mixed * conv_se).astype(bf16)
    grad_conv_se = (grad_mixed * query_se.astype(f32)).astype(bf16)
    rim_grad_se = from_right(grad_conv_se, se_taps - 1)
    grad_prod_se = depthwise(jnp.concatenate([grad_conv_se, rim_grad_se], axis=0), filter_se)
    grad_key_se = (grad_prod_se * value_path.astype(f32)).astype(bf16)
    grad_value = (grad_prod_se * key_se.astype(f32)).astype(bf16)
    local_filter_se = depthwise(pad_se, grad_conv_se)[::-1]
    grad_filter_se, grad_gain = lax.psum((local_filter_se, local_gain), "ctx")
    return (
        grad_value,
        grad_query_se,
        grad_key_se,
        grad_query_mr,
        grad_key_mr,
        grad_filter_se,
        grad_filter_mr,
        grad_gain,
    )


def solution(mesh):
    placed = (
        P("ctx", "tp"),
        P("ctx", "tp"),
        P("ctx", "tp"),
        P("ctx", "tp"),
        P("ctx", "tp"),
        P("ctx", "tp"),
        P("tp"),
        P(None, "tp"),
        P(None, "tp"),
    )
    return jax.shard_map(
        shards,
        mesh=mesh,
        in_specs=placed,
        out_specs=(
            P("ctx", "tp"),
            P("ctx", "tp"),
            P("ctx", "tp"),
            P("ctx", "tp"),
            P("ctx", "tp"),
            P(None, "tp"),
            P(None, "tp"),
            P("tp"),
        ),
        check_vma=False,
    )
```

profile of v0, /device:TPU:0, one launch (start us, length us, event | category | flops | bytes accessed | tf_op | source)
XLA Modules:
  0.0 204.9 jit_solution(2100728544891367380)
XLA Ops:
  7.2 0.0 copy-start.7
  7.2 0.0 copy-start.5
  7.2 0.0 copy-start.8
  7.2 0.0 all-reduce.6.cloned.1.call-start
  7.3 1.4 fusion.12
  8.7 2.4 %collective-permute-start = (bf16[6,2048]{1,0:T(8,128)(2,1)S(1)}, bf16[6,2048]{1,0:T(8,128)(2,1)S(1)}, u32[]{:S(2)}, u32[]{:S(2)}) collective-permute-start(bf16[6,2048]{1,0:T(8,128)(2,1)S(1)} %slice.20), channel_id=1, source_target_pairs={{0,4},{4,8},{8,12},{12,16},{16,20},{20,24},{24,28},{1,5},{5,9},{9,... | collective-permute-start | bytes 73736 | tf_op jit(solution)/shard_map/ppermute | solution.py:12
  11.1 0.9 fusion.14
  12.0 1.3 collective-permute-start.1
  13.3 0.4 rev.12
  13.8 5.2 %rev.13 = bf16[128,2048]{1,0:T(8,128)(2,1)} reverse(bf16[128,2048]{1,0:T(8,128)(2,1)S(1)} %copy-done.8), dimensions={0} | reverse | bytes 1048576 | tf_op jit(solution)/shard_map/rev | solution.py:66
  19.0 0.0 collective-permute-done
  19.0 0.1 maximum_bitcast_fusion.2
  19.1 0.8 copy-done.1
  20.0 0.0 copy-start.14
  20.0 0.2 reshape.20
  20.2 0.3 copy.28
  20.6 0.1 copy-done.14
  20.7 0.6 convolution_select_fusion.1
  21.3 0.7 copy.30
  22.0 0.0 copy-start.3
  22.0 0.1 reshape.24
  22.2 0.9 copy-done.3
  23.1 0.2 multiply_reduce_fusion.2
  23.3 12.9 %psum.35 = f32[128,1]{0,1:T(1,128)S(1)} all-reduce(f32[128,1]{0,1:T(1,128)S(1)} %bitcast.67), channel_id=1, replica_groups=mesh['ctx'=8,'tp'=4] {'tp'}, use_global_device_ids=true, to_apply=%region_1.0 | all-reduce | flops 128 | bytes 1024 | tf_op jit(solution)/shard_map/psum | solution.py:37
  36.2 0.0 collective-permute-done.1
  36.2 1.3 maximum_bitcast_fusion
  37.6 0.0 copy-start.4
  37.6 14.9 %fusion = f32[1,128,2048]{2,0,1:T(1,128)S(1)} fusion(bf16[1,255,2048]{2,1,0:T(8,128)(2,1)S(1)} %maximum_bitcast_fusion, bf16[128,1,2048]{2,0,1:T(8,128)(2,1)S(1)} %bitcast.62), kind=kOutput, calls=%fused_computation.2 | convolution fusion | flops 67108864 | bytes 2617344 | tf_op jit(solution)/shard_map/conv_general_dilated | solution.py:16
  52.5 0.0 copy-start
  52.5 2.3 %multiply_reduce_fusion = (f32[2048]{0:T(1024)}, f32[128]{0:T(128)S(1)}, bf16[128,2048]{1,0:T(8,128)(2,1)}, bf16[128,2048]{1,0:T(8,128)(2,1)S(1)}) fusion(f32[128,2048]{1,0:T(8,128)S(1)} %get-tuple-element.13, f32[128]{0:T(128)S(1)} %get-tuple-element.21, bf16[128,2048]{1,0:T(8,128)(2,1)S(1)} %copy-done.4, f32[1,128,2048]{2,0,1:T(1,128)S(1)} %fusion, ...), kind=kLoop, calls=%fused_computation.40 | loop fusion | flops 4192128 | bytes 3687424 | tf_op jit(solution)/shard_map/reduce_sum | solution.py:71
  54.8 8.3 %psum.36 = f32[128]{0:T(128)S(1)} all-reduce(f32[128]{0:T(128)S(1)} %get-tuple-element.9), channel_id=1, replica_groups=mesh['ctx'=8,'tp'=4] {'tp'}, use_global_device_ids=true, to_apply=%region_3.0 | all-reduce | flops 128 | bytes 1024 | tf_op jit(solution)/shard_map/psum | solution.py:37
  63.1 3.2 %multiply_convert_fusion.1 = (bf16[128,2048]{1,0:T(8,128)(2,1)}, bf16[128,2048]{1,0:T(8,128)(2,1)S(1)}) fusion(f32[1,136,2048]{2,1,0:T(8,128)S(1)} %reshape.24, f32[128]{0:T(128)S(1)} %psum.36, f32[128,2048]{1,0:T(8,128)S(1)} %get-tuple-element.13, f32[128]{0:T(128)S(1)} %get-tuple-element.20, f32[2048]{0:T(1024)S(1)} %convert_element_type.68, ...), kind=kLoop, calls=%fused_computation.42 | loop fusion | flops 3407872 | bytes 5252608 | tf_op jit(solution)/shard_map/convert_element_type | solution.py:74
  66.3 1.3 collective-permute-start.2
  67.6 2.3 %fusion.8 = f32[1,7,2048]{2,0,1:T(1,128)S(1)} fusion(bf16[1,134,2048]{2,1,0:T(8,128)(2,1)S(1)} %copy-done.2, bf16[128,1,2048]{2,0,1:T(8,128)(2,1)S(1)} %bitcast.61), kind=kOutput, calls=%fused_computation.21 | convolution fusion | flops 3670016 | bytes 1130496 | tf_op jit(solution)/shard_map/conv_general_dilated | solution.py:16
  69.9 4.8 %rev.14 = f32[7,2048]{1,0:T(8,128)} reverse(f32[7,2048]{1,0:T(8,128)S(1)} %bitcast.64), dimensions={0} | reverse | bytes 114688 | tf_op jit(solution)/shard_map/rev | solution.py:80
  74.8 0.9 slice.27
  75.7 3.8 %collective-permute-start.3 = (bf16[127,2048]{1,0:T(8,128)(2,1)}, bf16[127,2048]{1,0:T(8,128)(2,1)}, u32[]{:S(2)}, u32[]{:S(2)}) collective-permute-start(bf16[127,2048]{1,0:T(8,128)(2,1)} %slice.27), channel_id=1, source_target_pairs={{0,4},{4,8},{8,12},{12,16},{16,20},{20,24},{24,28},{1,5},{5,9},{9,... | collective-permute-start | bytes 1560584 | tf_op jit(solution)/shard_map/ppermute | solution.py:12
  79.5 0.0 all-reduce.6.cloned.1.call-update
  79.5 0.2 all-reduce.4.cloned.1.call-start
  79.8 0.0 collective-permute-done.2
  79.8 0.1 maximum_bitcast_fusion.3
  79.8 0.1 pad.2
  79.9 0.2 reshape.27
  80.1 0.3 copy.34
  80.5 0.6 convolution_select_fusion
  81.1 0.7 copy.36
  81.8 0.1 reshape.31
  82.0 2.4 %fusion.13 = (bf16[128,2048]{1,0:T(8,128)(2,1)}, bf16[128,2048]{1,0:T(8,128)(2,1)}) fusion(bf16[128,2048]{1,0:T(8,128)(2,1)} %param.9, f32[1,136,2048]{2,1,0:T(8,128)S(1)} %reshape.31, bf16[128,2048]{1,0:T(8,128)(2,1)} %param.10), kind=kLoop, calls=%fused_computation.26 | loop fusion | flops 1572864 | bytes 3145728 | tf_op jit(solution)/shard_map/convert_element_type | solution.py:78
  84.4 0.0 collective-permute-done.3
  84.4 1.2 maximum_bitcast_fusion.1
  85.6 14.6 %fusion.2 = f32[1,128,2048]{2,0,1:T(1,128)S(1)} fusion(bf16[1,255,2048]{2,1,0:T(8,128)(2,1)S(1)} %maximum_bitcast_fusion.1, bf16[128,1,2048]{2,0,1:T(8,128)(2,1)} %bitcast.16), kind=kOutput, calls=%fused_computation.4 | convolution fusion | flops 67108864 | bytes 2617344 | tf_op jit(solution)/shard_map/conv_general_dilated | solution.py:16
  100.2 0.3 copy.82
  100.5 0.0 copy-start.10
  100.5 5.2 %rev.15 = f32[128,2048]{1,0:T(8,128)} reverse(f32[128,2048]{1,0:T(8,128)S(1)} %bitcast.60), dimensions={0} | reverse | bytes 2097152 | tf_op jit(solution)/shard_map/rev | solution.py:69
  105.7 0.0 all-reduce.4.cloned.1.call-update
  105.8 0.0 copy-start.6
  105.8 14.9 %fusion.4 = f32[1,128,2048]{2,0,1:T(1,128)S(1)} fusion(bf16[1,255,2048]{2,1,0:T(8,128)(2,1)S(1)} %maximum_bitcast_fusion.1, bf16[128,1,2048]{2,0,1:T(8,128)(2,1)S(1)} %bitcast.63), kind=kOutput, calls=%fused_computation.6 | convolution fusion | flops 67108864 | bytes 2617344 | tf_op jit(solution)/shard_map/conv_general_dilated | solution.py:16
  120.7 1.1 fusion.15
  121.8 9.9 %all-reduce.6.cloned.1.call-done = (f32[7,2048]{1,0:T(8,128)}, f32[2048]{0:T(1024)}) async-done(((f32[7,2048]{1,0:T(8,128)}, f32[2048]{0:T(1024)}), (f32[7,2048]{1,0:T(8,128)}, f32[2048]{0:T(1024)})) %all-reduce.6.cloned.1.call-update) | async-done | bytes 65552 | tf_op jit(solution)/shard_map/psum | solution.py:81
  131.7 62.0 %all-reduce.4.cloned.1.call-done = f32[128,2048]{1,0:T(8,128)} async-done(((f32[128,2048]{1,0:T(8,128)}), f32[128,2048]{1,0:T(8,128)}) %all-reduce.4.cloned.1.call-update) | async-done | bytes 1048592 | tf_op jit(solution)/shard_map/psum | solution.py:70
  193.7 1.5 copy.87
  195.1 2.3 %copy.88 = f32[128,2048]{1,0:T(8,128)} copy(f32[128,2048]{1,0:T(8,128)} %all-reduce.4.cloned.1.call-done) | data formatting | bytes 2097152
  197.4 0.0 copy-done.12
  197.4 0.6 copy.89
  (25 shorter events, 0.2 us)
Async XLA Ops:
  7.2 3.9 %copy-start.7 = (bf16[128,2048]{1,0:T(8,128)(2,1)S(1)}, bf16[128,2048]{1,0:T(8,128)(2,1)}, u32[]{:S(2)}) copy-start(bf16[128,2048]{1,0:T(8,128)(2,1)} %param.13) | copy-start | bytes 1572868
  7.2 3.9 %copy-start.5 = (bf16[128,2048]{1,0:T(8,128)(2,1)S(1)}, bf16[128,2048]{1,0:T(8,128)(2,1)}, u32[]{:S(2)}) copy-start(bf16[128,2048]{1,0:T(8,128)(2,1)} %param.14) | copy-start | bytes 1572868
  7.2 6.1 %copy-start.11 = (bf16[7,2048]{1,0:T(8,128)(2,1)S(1)}, bf16[7,2048]{1,0:T(8,128)(2,1)}, u32[]{:S(2)}) copy-start(bf16[7,2048]{1,0:T(8,128)(2,1)} %param.16) | copy-start | bytes 86020
  7.2 6.6 %copy-start.13 = (bf16[2048]{0:T(1024)(128)(2,1)S(1)}, bf16[2048]{0:T(1024)(128)(2,1)}, u32[]{:S(2)}) copy-start(bf16[2048]{0:T(1024)(128)(2,1)} %param.15) | copy-start | bytes 12292
  7.2 6.6 %copy-start.8 = (bf16[128,2048]{1,0:T(8,128)(2,1)S(1)}, bf16[128,2048]{1,0:T(8,128)(2,1)}, u32[]{:S(2)}) copy-start(bf16[128,2048]{1,0:T(8,128)(2,1)} %param.17) | copy-start | bytes 1572868
  7.2 124.5 %all-reduce.6.cloned.1.call-start = ((), (), s32[]{:S(2)}) async-start(), calls=%async_computation.1 | async-start | bytes 147456 | tf_op jit(solution)/shard_map/psum | solution.py:81
  8.7 10.3 %collective-permute-start = (bf16[6,2048]{1,0:T(8,128)(2,1)S(1)}, bf16[6,2048]{1,0:T(8,128)(2,1)S(1)}, u32[]{:S(2)}, u32[]{:S(2)}) collective-permute-start(bf16[6,2048]{1,0:T(8,128)(2,1)S(1)} %slice.20), channel_id=1, source_target_pairs={{0,4},{4,8},{8,12},{12,16},{16,20},{20,24},{24,28},{1,5},{5,9},{9,... | collective-permute-start | bytes 73736 | tf_op jit(solution)/shard_map/ppermute | solution.py:12
  12.0 24.2 %collective-permute-start.1 = (bf16[127,2048]{1,0:T(8,128)(2,1)}, bf16[127,2048]{1,0:T(8,128)(2,1)}, u32[]{:S(2)}, u32[]{:S(2)}) collective-permute-start(bf16[127,2048]{1,0:T(8,128)(2,1)} %bitcast.59), channel_id=1, source_target_pairs={{4,0},{8,4},{12,8},{16,12},{20,16},{24,20},{28,24},{5,1},{9,5},{13... | collective-permute-start | bytes 1560584 | tf_op jit(solution)/shard_map/ppermute | solution.py:12
  19.1 0.8 copy-start.1
  20.0 0.7 copy-start.14
  22.0 1.0 copy-start.3
  23.3 14.3 %copy-start.9 = (bf16[128,2048]{1,0:T(8,128)(2,1)S(1)}, bf16[128,2048]{1,0:T(8,128)(2,1)}, u32[]{:S(2)}) copy-start(bf16[128,2048]{1,0:T(8,128)(2,1)} %param.17) | copy-start | bytes 1572868
  37.6 14.9 %copy-start.4 = (bf16[128,2048]{1,0:T(8,128)(2,1)S(1)}, bf16[128,2048]{1,0:T(8,128)(2,1)}, u32[]{:S(2)}) copy-start(bf16[128,2048]{1,0:T(8,128)(2,1)} %param.12) | copy-start | bytes 1572868
  52.5 2.3 %copy-start = (f32[1,128,2048]{2,0,1:T(1,128)}, f32[1,128,2048]{2,0,1:T(1,128)S(1)}, u32[]{:S(2)}) copy-start(f32[1,128,2048]{2,0,1:T(1,128)S(1)} %fusion) | copy-start | bytes 3145732
  63.1 4.5 %copy-start.2 = (bf16[1,134,2048]{2,1,0:T(8,128)(2,1)S(1)}, bf16[1,134,2048]{2,1,0:T(8,128)(2,1)}, u32[]{:S(2)}) copy-start(bf16[1,134,2048]{2,1,0:T(8,128)(2,1)} %copy-done.1) | copy-start | bytes 1646596
  66.3 13.5 %collective-permute-start.2 = (bf16[6,2048]{1,0:T(8,128)(2,1)S(1)}, bf16[6,2048]{1,0:T(8,128)(2,1)S(1)}, u32[]{:S(2)}, u32[]{:S(2)}) collective-permute-start(bf16[6,2048]{1,0:T(8,128)(2,1)S(1)} %slice.24), channel_id=1, source_target_pairs={{4,0},{8,4},{12,8},{16,12},{20,16},{24,20},{28,24},{5,1},{9,5},{13... | collective-permute-start | bytes 73736 | tf_op jit(solution)/shard_map/ppermute | solution.py:12
  75.7 8.7 %collective-permute-start.3 = (bf16[127,2048]{1,0:T(8,128)(2,1)}, bf16[127,2048]{1,0:T(8,128)(2,1)}, u32[]{:S(2)}, u32[]{:S(2)}) collective-permute-start(bf16[127,2048]{1,0:T(8,128)(2,1)} %slice.27), channel_id=1, source_target_pairs={{0,4},{4,8},{8,12},{12,16},{16,20},{20,24},{24,28},{1,5},{5,9},{9,... | collective-permute-start | bytes 1560584 | tf_op jit(solution)/shard_map/ppermute | solution.py:12
  79.5 114.1 %all-reduce.4.cloned.1.call-start = ((), (), s32[]{:S(2)}) async-start(), calls=%async_computation | async-start | bytes 2097152 | tf_op jit(solution)/shard_map/psum | solution.py:70
  100.5 5.2 %copy-start.10 = (bf16[128,2048]{1,0:T(8,128)(2,1)S(1)}, bf16[128,2048]{1,0:T(8,128)(2,1)}, u32[]{:S(2)}) copy-start(bf16[128,2048]{1,0:T(8,128)(2,1)} %rev.13) | copy-start | bytes 1572868
  105.8 14.9 %copy-start.6 = (bf16[128,2048]{1,0:T(8,128)(2,1)S(1)}, bf16[128,2048]{1,0:T(8,128)(2,1)}, u32[]{:S(2)}) copy-start(bf16[128,2048]{1,0:T(8,128)(2,1)} %param.14) | copy-start | bytes 1572868
  131.7 65.7 %copy-start.12 = (f32[2048]{0:T(1024)S(1)}, f32[2048]{0:T(1024)}, u32[]{:S(2)}) copy-start(f32[2048]{0:T(1024)} %get-tuple-element.29) | copy-start | bytes 24580
Sparse Core Ops, SparseCore 0:
  79.7 51.9 all-reduce.5
  135.8 57.8 all-reduce.3
where the time goes:
time: 205 us
  waiting for transfers between devices  71.9 us (35%)
  matrix products  47.8 us (23%)
  local copies, waits for them, and re-layouts  26.1 us (13%)
  blocking collectives  21.3 us (10%)
  between operations  14.5 us (7%)
  other arithmetic  14.3 us (7%)
  starting transfers between devices  9.01 us (4%)
    psum x1, waiting for transfers between devices, shards(): grad_filter_mr = lax.psum(local_filter_mr, 'ctx')  62 us
    conv_general_dilated x6, matrix products, depthwise(): lax.conv_general_dilated(lhs[None], kernel[:, None, :], (1,), 'VALID', di...  47.8 us
    psum x2, blocking collectives, token_total(): return lax.psum(partial_sum, 'tp')  21.3 us
    psum x1, waiting for transfers between devices, shards(): grad_filter_se, grad_gain = lax.psum((local_filter_se, local_gain), 'ctx')  9.91 us
    ppermute x4, starting transfers between devices, shifted(): return lax.ppermute(block, axis, route)  8.75 us
    unnamed x35, local copies, waits for them, and re-layouts  6.58 us
    rev x1, local copies, waits for them, and re-layouts, shards(): local_filter_mr = depthwise(pad_mr, grad_conv_mr)[::-1]  5.19 us
    rev x1, local copies, waits for them, and re-layouts, shards(): conv_mr = depthwise(pad_mr, filter_mr[::-1])  5.18 us
  transfers between devices with their start and end apart: 6, of which 2 were waited for; matrix products, arithmetic and copies ran while one was open for 29% of the time, Pallas kernels for 0%

commit v1 on v0

v1 whole, which is shorter than its diff:
```python
import functools
import math

import jax
import jax.numpy as jnp
import ml_dtypes
import numpy as np
from jax import lax
from jax.experimental import pallas as pl
from jax.experimental.pallas import tpu as pltpu
from jax.sharding import PartitionSpec as P

D = 8192
CW = 256
PIECES = 4
F32 = jnp.float32
BF16 = jnp.bfloat16


def split(m):
    hi = m.astype(ml_dtypes.bfloat16)
    lo = (m - hi.astype(np.float64)).astype(ml_dtypes.bfloat16)
    return hi, lo


def matrices(rows):
    n = 2 * rows
    theta = 2.0 * math.pi * (np.arange(rows) + 0.5) / n
    ang = theta[:, None] * np.arange(n)[None, :]
    fwd = np.concatenate([np.cos(ang), -np.sin(ang)], axis=0)
    bwd = np.concatenate([np.cos(ang).T, -np.sin(ang).T], axis=1) / rows
    fh, fl = split(fwd)
    near = np.concatenate([fh[:, :rows], fl[:, :rows]], axis=1)
    far = np.concatenate([fh[:, rows:], fl[:, rows:]], axis=1)
    bh, bl = split(bwd)
    return np.stack([fh, fl, near, far, bh, bl])


def body(
    n, ntp, fused, eps,
    vp, ks, qs, km, qm, og, gain, fse, fmr, mats,
    o_val, o_qse, o_kse, o_qmr, o_kmr, o_small, o_fmr,
    win_se, g2, wsend, wh, conv, fs, os_, gp, win_gs, acc, row_send, row_recv, inv_send, invl_row, inv2, invl2, k2,
    pfb, own, rc, sx, rx, ag_own, ag_x, ag_c, sm, rs_s, ag_s,
    tail_sem, gh_s, gh_r, wh_s, wh_r, row_s, row_r, inv_sem, gs_sem,
    rc_s, rc_r, rx_s, rx_r, agx_s, agx_r, agc_s, agc_r, rss_s, rss_r, ags_s, ags_r,
):
    me = lax.axis_index("ctx")
    tp = lax.axis_index("tp")
    rows, chans = vp.shape
    taps = fse.shape[0]
    nc = chans // CW
    hc = chans // PIECES
    per = hc // CW
    has_l = me > 0
    has_r = me < n - 1
    left = (me + n - 1) % n
    right = (me + 1) % n
    mesh_ids = pl.DeviceIdType.MESH

    def remote(src, dst, ssem, rsem, where):
        return pltpu.make_async_remote_copy(
            src_ref=src, dst_ref=dst, send_sem=ssem, recv_sem=rsem, device_id=where, device_id_type=mesh_ids
        )

    def lanes(c):
        return pl.ds(pl.multiple_of(c * CW, CW), CW)

    def wide(ref):
        return jnp.concatenate([ref[...]] * (CW // 128), axis=1)

    bar = pltpu.get_barrier_semaphore()
    ctx_peers = [(me + d) % n for d in range(1, n)] if fused else [left, right]
    for p in ctx_peers:
        pl.semaphore_signal(bar, inc=1, device_id={"ctx": p}, device_id_type=mesh_ids)
    for d in range(1, ntp):
        pl.semaphore_signal(bar, inc=1, device_id={"tp": (tp + d) % ntp}, device_id_type=mesh_ids)

    @pl.when(jnp.logical_not(has_l))
    def _():
        win_se[pl.ds(0, 8), :] = jnp.zeros((8, chans), F32)
        wh[...] = jnp.zeros_like(wh)
        invl_row[...] = jnp.zeros_like(invl_row)

    @pl.when(jnp.logical_not(has_r))
    def _():
        g2[pl.ds(rows, rows), :] = jnp.zeros((rows, chans), BF16)
        win_gs[pl.ds(rows, 8), :] = jnp.zeros((8, chans), F32)

    @pl.loop(0, nc)
    def _(c):
        ch = lanes(c)
        win_se[pl.ds(8, rows), ch] = (ks[:, ch].astype(F32) * vp[:, ch].astype(F32)).astype(BF16).astype(F32)
        g2[pl.ds(0, rows), ch] = (og[:, ch].astype(F32) * qm[:, ch].astype(F32)).astype(BF16)

    pl.semaphore_wait(bar, len(ctx_peers) + ntp - 1)

    tail = remote(win_se.at[pl.ds(rows, 8)], win_se.at[pl.ds(0, 8)], tail_sem.at[0], tail_sem.at[1], {"ctx": right})

    def g_piece(h):
        hl = pl.ds(pl.multiple_of(h * hc, hc), hc)
        return remote(g2.at[pl.ds(0, rows), hl], g2.at[pl.ds(rows, rows), hl], gh_s.at[h], gh_r.at[h], {"ctx": left})

    def w_piece(h):
        hl = pl.ds(pl.multiple_of(h * hc, hc), hc)
        return remote(wsend.at[:, hl], wh.at[:, hl], wh_s.at[h], wh_r.at[h], {"ctx": right})

    @pl.when(has_r)
    def _():
        tail.start()

    @pl.when(has_l)
    def _():
        for h in range(PIECES):
            g_piece(h).start()
        tail.wait_recv()

    acc[...] = jnp.zeros_like(acc)

    def fold(x):
        s = x[:, :128]
        for i in range(1, CW // 128):
            s = s + x[:, i * 128 : (i + 1) * 128]
        return s

    @pl.loop(0, PIECES)
    def _(h):
        for i in range(per):
            ch = lanes(h * per + i)
            f = fse[:, ch].astype(F32)
            cs = win_se[pl.ds(8, rows), ch] * f[0:1]
            for j in range(1, taps):
                cs = cs + win_se[pl.ds(8 - j, rows), ch] * f[j : j + 1]
            conv[:, ch] = cs
            mixed = qs[:, ch].astype(F32) * cs
            acc[...] += fold(mixed * mixed)
            wsend[:, ch] = (mixed * gain[:, ch] * km[:, ch].astype(F32)).astype(BF16)

        @pl.when(has_r)
        def _():
            w_piece(h).start()

    def share(k):
        row_send[k] = jnp.broadcast_to(jnp.sum(acc[...].T, axis=0, keepdims=True), (8, 128))
        for d in range(1, ntp):
            row_copy(k, d).start()

    def row_copy(k, d):
        return remote(
            row_send.at[k], row_recv.at[k, d - 1], row_s.at[k, d - 1], row_r.at[k, d - 1], {"tp": (tp + d) % ntp}
        )

    def gather(k):
        for d in range(1, ntp):
            row_copy(k, d).wait()
        total = row_send[k]
        for d in range(1, ntp):
            total = total + row_recv[k, d - 1]
        return total

    share(0)

    def twice(x):
        return jnp.concatenate([x, x], axis=0)

    def dot(a, b):
        return jnp.dot(a, b, preferred_element_type=F32)

    def back(y, at):
        hi = y.astype(BF16)
        lo = (y - hi.astype(F32)).astype(BF16)
        bh = mats[4, pl.ds(at, rows), :]
        bl = mats[5, pl.ds(at, rows), :]
        return dot(bh, hi) + (dot(bl, hi) + dot(bh, lo))

    @pl.loop(0, nc)
    def _(c):
        ch = lanes(c)
        fs[:, ch] = dot(mats[2], twice(fmr[:, ch]))
        os_[:, ch] = dot(mats[2], twice(g2[pl.ds(0, rows), ch]))

    inv_row = lax.rsqrt(gather(0) / D + 1e-06)
    inv_send[...] = inv_row
    inv_copy = remote(inv_send, invl_row, inv_sem.at[0], inv_sem.at[1], {"ctx": right})

    @pl.when(has_r)
    def _():
        inv_copy.start()

    inv2[...] = jnp.broadcast_to(inv_row[0:1], (128, 128)).T

    acc[...] = jnp.zeros_like(acc)

    @pl.loop(0, PIECES)
    def _(h):
        @pl.when(has_l)
        def _():
            g_piece(h).wait_send()

        @pl.when(has_r)
        def _():
            g_piece(h).wait_recv()

        for i in range(per):
            ch = lanes(h * per + i)
            g = os_[:, ch] + dot(mats[3], twice(g2[pl.ds(rows, rows), ch]))
            gr, gi = g[:rows], g[rows:]
            fr, fi = fs[pl.ds(0, rows), ch], fs[pl.ds(rows, rows), ch]
            grad = back(jnp.concatenate([gr * fr + gi * fi, gi * fr - gr * fi], axis=0), 0)
            gp[:, ch] = grad
            mixed = qs[:, ch].astype(F32) * conv[:, ch]
            normed = (mixed * wide(inv2) * gain[:, ch]).astype(BF16)
            o_kmr[:, ch] = (grad * normed.astype(F32)).astype(BF16)
            acc[...] += fold(grad * km[:, ch].astype(F32) * gain[:, ch] * mixed)

    share(1)

    @pl.when(has_l)
    def _():
        inv_copy.wait_recv()
        for h in range(PIECES):
            w_piece(h).wait_recv()

    invl2[...] = jnp.broadcast_to(invl_row[0:1], (128, 128)).T

    def medium(c):
        ch = lanes(c)
        kmf = km[:, ch].astype(F32)
        mixed = qs[:, ch].astype(F32) * conv[:, ch]
        normed = (mixed * wide(inv2) * gain[:, ch]).astype(BF16)
        prod = (kmf * normed.astype(F32)).astype(BF16)
        halo = (wh[:, ch].astype(F32) * wide(invl2)).astype(BF16)
        window = jnp.concatenate([halo, prod], axis=0)
        x = dot(mats[0], window) + dot(mats[1], window)
        xr, xi = x[:rows], x[rows:]
        gr, gi = os_[pl.ds(0, rows), ch], os_[pl.ds(rows, rows), ch]
        fr, fi = fs[pl.ds(0, rows), ch], fs[pl.ds(rows, rows), ch]
        part = -back(jnp.concatenate([gr * xr + gi * xi, gi * xr - gr * xi], axis=0), rows)
        y = back(jnp.concatenate([xr * fr - xi * fi, xr * fi + xi * fr], axis=0), rows)
        o_qmr[:, ch] = (og[:, ch].astype(F32) * y).astype(BF16)
        return part

    if fused:
        chips = n // 2
        core = me % 2
        chip = me // 2
        mate = me + 1 - 2 * core

        def to_mate(i):
            return remote(pfb.at[i], rc.at[i], rc_s.at[i], rc_r.at[i], {"ctx": mate})

        def to_chip(d):
            return remote(
                sx.at[d - 1], rx.at[d - 1], rx_s.at[d - 1], rx_r.at[d - 1], {"ctx": ((chip + d) % chips) * 2 + core}
            )

        def all_chip(d):
            return remote(
                ag_own, ag_x.at[d - 1], agx_s.at[d - 1], agx_r.at[d - 1], {"ctx": ((chip + d) % chips) * 2 + core}
            )

        def all_mate(d):
            src = ag_own if d == 0 else ag_x.at[d - 1]
            return remote(src, ag_c.at[d], agc_s.at[d], agc_r.at[d], {"ctx": mate})

        @pl.loop(0, chips)
        def _(i):
            pfb[i] = medium(2 * i + 1 - core).astype(BF16)
            to_mate(i).start()

        @pl.loop(0, chips)
        def _(i):
            own[i] = medium(2 * i + core)

        for d in range(1, chips):
            to = (chip + d) % chips
            to_mate(to).wait_recv()
            sx[d - 1] = (own[to] + rc[to].astype(F32)).astype(BF16)
            to_chip(d).start()
    else:

        @pl.loop(0, nc)
        def _(c):
            o_fmr[:, lanes(c)] = medium(c).astype(o_fmr.dtype)

    dot_row = gather(1)
    inv = inv2[...]
    k2[...] = inv * inv * inv * jnp.broadcast_to(dot_row[0:1], (128, 128)).T / D

    @pl.loop(0, nc)
    def _(c):
        ch = lanes(c)
        cs = conv[:, ch]
        q = qs[:, ch].astype(F32)
        mixed = q * cs
        inv_w = wide(inv2)
        grad_normed = gp[:, ch] * km[:, ch].astype(F32)
        grad_mixed = inv_w * (grad_normed * gain[:, ch]) - mixed * wide(k2)
        o_qse[:, ch] = (grad_mixed * cs).astype(BF16)
        gcs = (grad_mixed * q).astype(BF16).astype(F32)
        win_gs[pl.ds(0, rows), ch] = gcs
        for j in range(taps):
            sm[c, pl.ds(j, 1), :] = jnp.sum(gcs * win_se[pl.ds(8 - j, rows), ch], axis=0, keepdims=True)
        sm[c, pl.ds(taps, 1), :] = jnp.sum(grad_normed * mixed * inv_w, axis=0, keepdims=True)

    head = remote(win_gs.at[pl.ds(0, 8)], win_gs.at[pl.ds(rows, 8)], gs_sem.at[0], gs_sem.at[1], {"ctx": left})

    @pl.when(has_l)
    def _():
        head.start()

    if fused:

        def small_to(d):
            return remote(
                sm.at[(me + d) % n], rs_s.at[d - 1], rss_s.at[d - 1], rss_r.at[d - 1], {"ctx": (me + d) % n}
            )

        def small_all(d):
            return remote(
                ag_s.at[0], ag_s.at[d], ags_s.at[d - 1], ags_r.at[d - 1], {"ctx": (me + d) % n}
            )

        for d in range(1, n):
            small_to(d).start()

        to_mate(chip).wait_recv()
        total = own[chip] + rc[chip].astype(F32)
        for d in range(1, chips):
            to_chip(d).wait_recv()
            total = total + rx[d - 1].astype(F32)
        ag_own[...] = total.astype(BF16)
        for d in range(1, chips):
            all_chip(d).start()
        all_mate(0).start()

        total_s = sm[me]
        for d in range(1, n):
            small_to(d).wait_recv()
            total_s = total_s + rs_s[d - 1]
        ag_s[0] = total_s
        for d in range(1, n):
            small_all(d).start()

    @pl.when(has_r)
    def _():
        head.wait_recv()

    @pl.loop(0, nc)
    def _(c):
        ch = lanes(c)
        f = fse[:, ch].astype(F32)
        g = win_gs[pl.ds(0, rows), ch] * f[0:1]
        for j in range(1, taps):
            g = g + win_gs[pl.ds(j, rows), ch] * f[j : j + 1]
        o_kse[:, ch] = (g * vp[:, ch].astype(F32)).astype(BF16)
        o_val[:, ch] = (g * ks[:, ch].astype(F32)).astype(BF16)

    if fused:
        for d in range(1, chips):
            all_chip(d).wait_recv()
            all_mate(d).start()
        o_fmr[:, lanes(me)] = ag_own[...]
        for d in range(1, chips):
            o_fmr[:, lanes(((chip + chips - d) % chips) * 2 + core)] = ag_x[d - 1]
        o_small[:, lanes(me)] = ag_s[0]
        for d in range(1, n):
            small_all(d).wait_recv()
            o_small[:, lanes((me + n - d) % n)] = ag_s[d]
        for d in range(chips):
            all_mate(d).wait_recv()
            o_fmr[:, lanes(((chip + chips - d) % chips) * 2 + 1 - core)] = ag_c[d]
        for i in range(chips):
            to_mate(i).wait_send()
            all_mate(i).wait_send()
        for d in range(1, chips):
            to_chip(d).wait_send()
            all_chip(d).wait_send()
        for d in range(1, n):
            small_to(d).wait_send()
            small_all(d).wait_send()
    else:

        @pl.loop(0, nc)
        def _(c):
            o_small[:, lanes(c)] = sm[c]

    @pl.when(has_l)
    def _():
        head.wait_send()

    @pl.when(has_r)
    def _():
        tail.wait_send()
        inv_copy.wait_send()
        for h in range(PIECES):
            w_piece(h).wait_send()


def shards(n, ntp, vp, ks, qs, km, qm, og, norm_gain, fse, fmr):
    rows, chans = vp.shape
    taps = fse.shape[0]
    nc = chans // CW
    fused = n == nc and n % 2 == 0
    chips = max(n // 2, 2) if fused else 2
    blk = (rows, CW)
    peers = n if fused else 2
    wide_out = jax.ShapeDtypeStruct((rows, chans), BF16)
    dma = pltpu.SemaphoreType.DMA
    vmem = pltpu.VMEM
    scratch = [
        vmem((rows + 8, chans), F32),
        vmem((2 * rows, chans), BF16),
        vmem((rows, chans), BF16),
        vmem((rows, chans), BF16),
        vmem((rows, chans), F32),
        vmem((2 * rows, chans), F32),
        vmem((2 * rows, chans), F32),
        vmem((rows, chans), F32),
        vmem((rows + 8, chans), F32),
        vmem((rows, 128), F32),
        vmem((2, 8, 128), F32),
        vmem((2, ntp - 1, 8, 128), F32),
        vmem((8, 128), F32),
        vmem((8, 128), F32),
        vmem((rows, 128), F32),
        vmem((rows, 128), F32),
        vmem((rows, 128), F32),
        vmem((chips,) + blk, BF16),
        vmem((chips,) + blk, F32),
        vmem((chips,) + blk, BF16),
        vmem((chips - 1,) + blk, BF16),
        vmem((chips - 1,) + blk, BF16),
        vmem(blk, BF16),
        vmem((chips - 1,) + blk, BF16),
        vmem((chips,) + blk, BF16),
        vmem((nc, taps + 1, CW), F32),
        vmem((peers - 1, taps + 1, CW), F32),
        vmem((peers, taps + 1, CW), F32),
        dma((2,)),
        dma((PIECES,)), dma((PIECES,)),
        dma((PIECES,)), dma((PIECES,)),
        dma((2, ntp - 1)), dma((2, ntp - 1)),
        dma((2,)),
        dma((2,)),
        dma((chips,)), dma((chips,)),
        dma((chips - 1,)), dma((chips - 1,)),
        dma((chips - 1,)), dma((chips - 1,)),
        dma((chips,)), dma((chips,)),
        dma((peers - 1,)), dma((peers - 1,)),
        dma((peers - 1,)), dma((peers - 1,)),
    ]
    spec = pl.BlockSpec(memory_space=pltpu.VMEM)
    mats = jnp.asarray(matrices(rows))
    outs = pl.pallas_call(
        functools.partial(body, n, ntp, fused, 1e-06),
        out_shape=[wide_out] * 5
        + [jax.ShapeDtypeStruct((taps + 1, chans), F32), jax.ShapeDtypeStruct((rows, chans), BF16 if fused else F32)],
        in_specs=[spec] * 10,
        out_specs=[spec] * 7,
        scratch_shapes=scratch,
        compiler_params=pltpu.CompilerParams(
            collective_id=0, has_side_effects=True, vmem_limit_bytes=48 * 1024 * 1024
        ),
        name="hyena_backward",
    )(vp, ks, qs, km, qm, og, norm_gain.astype(F32).reshape(1, chans), fse, fmr, mats)
    o_val, o_qse, o_kse, o_qmr, o_kmr, small, gf = outs
    if not fused:
        small, gf = lax.psum((small, gf), "ctx")
    return o_val, o_qse, o_kse, o_qmr, o_kmr, small[:taps], gf.astype(F32), small[taps]


def solution(mesh):
    tok = P("ctx", "tp")
    fil = P(None, "tp")
    return jax.shard_map(
        functools.partial(shards, mesh.shape["ctx"], mesh.shape["tp"]),
        mesh=mesh,
        in_specs=(tok,) * 6 + (P("tp"), fil, fil),
        out_specs=(tok,) * 5 + (fil, fil, P("tp")),
        check_vma=False,
    )
```

time: 205 us -> 51.5 us (0.25)
  waiting for transfers between devices: 71.9 us -> 0 us
  matrix products: 47.8 us -> 0 us
  Pallas kernels: 0 us -> 37.4 us
  blocking collectives: 21.3 us -> 0 us
  local copies, waits for them, and re-layouts: 26.1 us -> 11.2 us
  between operations: 14.5 us -> 0.65 us
  other arithmetic: 14.3 us -> 1.76 us
  starting transfers between devices: 9.01 us -> 0 us
    psum x2 -> x0, waiting for transfers between devices: 71.9 us -> none  [the longest x1 62 us: shards(): grad_filter_mr = lax.psum(local_filter_mr, 'ctx')]
    conv_general_dilated x6 -> x0, matrix products: 47.8 us -> none  [depthwise(): lax.conv_general_dilated(lhs[None], kernel[:, None, :], (1,), 'VALID', di...]
    pallas_call x0 -> x1, Pallas kernels: none -> 37.4 us  [shards(): pl.pallas_call(functools.partial(body, n, ntp, fused, 1e-06), out_shape=[...]
    psum x2 -> x0, blocking collectives: 21.3 us -> none  [token_total(): return lax.psum(partial_sum, 'tp')]
    rev x4 -> x0, local copies, waits for them, and re-layouts: 15.6 us -> none  [the longest x1 5.19 us: shards(): local_filter_mr = depthwise(pad_mr, grad_conv_mr)[::-1]]
    ppermute x4 -> x0, starting transfers between devices: 8.75 us -> none  [shifted(): return lax.ppermute(block, axis, route)]
    convert_element_type x6 -> x1, other arithmetic: 9.1 us -> 1.07 us  [shards(): gf.astype(F32)]
    unnamed x35 -> x18, local copies, waits for them, and re-layouts: 6.58 us -> 10.6 us
  transfers between devices with their start and end apart: 6 -> 0, of which waited for: 2 -> 0; matrix products, arithmetic and copies ran while one was open for 29% -> 0% of each run, Pallas kernels for 0% -> 0%
where the time goes in v1:
time: 51.5 us; the launch traced here: 51 us
  Pallas kernels  37.4 us (73%)
  local copies, waits for them, and re-layouts  11.2 us (22%)
  other arithmetic  1.76 us (3%)
  between operations  0.65 us (1%)
    pallas_call x1, Pallas kernels, shards(): pl.pallas_call(functools.partial(body, n, ntp, fused, 1e-06), out_shape=[...  37.4 us
    unnamed x18, local copies, waits for them, and re-layouts  10.6 us
    convert_element_type x1, other arithmetic, shards(): gf.astype(F32)  1.07 us

profile of v1, /device:TPU:0, one launch (start us, length us, event | category | flops | bytes accessed | tf_op | source)
XLA Modules:
  0.0 51.0 jit_solution(3889431798901373420)
XLA Ops:
  0.6 0.7 %reshape.23 = f32[2048]{0:T(1024)S(1)} convert(bf16[2048]{0:T(1024)(128)(2,1)} %param.16) | non-fusion elementwise | flops 2048 | bytes 12288 | tf_op jit(solution)/shard_map/reshape | solution.py:466
  1.3 0.0 copy-start
  1.3 1.0 %copy-done = bf16[128,2048]{1,0:T(8,128)(2,1)S(1)} copy-done((bf16[128,2048]{1,0:T(8,128)(2,1)S(1)}, bf16[128,2048]{1,0:T(8,128)(2,1)}, u32[]{:S(2)}) %copy-start) | copy-done | bytes 524312
  2.4 0.0 copy-start.1
  2.4 1.0 %copy-done.1 = bf16[128,2048]{1,0:T(8,128)(2,1)S(1)} copy-done((bf16[128,2048]{1,0:T(8,128)(2,1)S(1)}, bf16[128,2048]{1,0:T(8,128)(2,1)}, u32[]{:S(2)}) %copy-start.1) | copy-done | bytes 524312
  3.4 0.0 copy-start.2
  3.4 1.0 %copy-done.2 = bf16[128,2048]{1,0:T(8,128)(2,1)S(1)} copy-done((bf16[128,2048]{1,0:T(8,128)(2,1)S(1)}, bf16[128,2048]{1,0:T(8,128)(2,1)}, u32[]{:S(2)}) %copy-start.2) | copy-done | bytes 524312
  4.4 0.0 copy-start.3
  4.5 1.0 %copy-done.3 = bf16[128,2048]{1,0:T(8,128)(2,1)S(1)} copy-done((bf16[128,2048]{1,0:T(8,128)(2,1)S(1)}, bf16[128,2048]{1,0:T(8,128)(2,1)}, u32[]{:S(2)}) %copy-start.3) | copy-done | bytes 524312
  5.5 0.0 copy-start.4
  5.5 1.0 %copy-done.4 = bf16[128,2048]{1,0:T(8,128)(2,1)S(1)} copy-done((bf16[128,2048]{1,0:T(8,128)(2,1)S(1)}, bf16[128,2048]{1,0:T(8,128)(2,1)}, u32[]{:S(2)}) %copy-start.4) | copy-done | bytes 524312
  6.5 0.0 copy-start.5
  6.5 0.8 %copy-done.5 = bf16[7,2048]{1,0:T(8,128)(2,1)S(1)} copy-done((bf16[7,2048]{1,0:T(8,128)(2,1)S(1)}, bf16[7,2048]{1,0:T(8,128)(2,1)}, u32[]{:S(2)}) %copy-start.5) | copy-done | bytes 28696
  7.3 37.4 %hyena_backward.1 = (bf16[128,2048]{1,0:T(8,128)(2,1)S(1)}, bf16[128,2048]{1,0:T(8,128)(2,1)S(1)}, bf16[128,2048]{1,0:T(8,128)(2,1)S(1)}, bf16[128,2048]{1,0:T(8...) custom-call(bf16[128,2048]{1,0:T(8,128)(2,1)S(1)} %copy-done, ...), custom_call_target="tpu_custom_call" | custom-call | tf_op jit(solution)/shard_map/hyena_backward/pallas_call | solution.py:455
  44.7 0.6 %slice.7 = f32[1,2048]{1,0:T(1,128)} slice(f32[8,2048]{1,0:T(8,128)S(1)} %get-tuple-element.20), slice={[7:8], [0:2048]} | slice | bytes 16384 | tf_op jit(solution)/shard_map/slice | solution.py:470
  45.3 1.1 %convert_element_type.4 = f32[128,2048]{1,0:T(8,128)} convert(bf16[128,2048]{1,0:T(8,128)(2,1)S(1)} %get-tuple-element.21) | non-fusion elementwise | flops 262144 | bytes 1572864 | tf_op jit(solution)/shard_map/convert_element_type | solution.py:470
  46.4 0.8 %copy.24 = bf16[128,2048]{1,0:T(8,128)(2,1)} copy(bf16[128,2048]{1,0:T(8,128)(2,1)S(1)} %get-tuple-element.30) | data formatting | bytes 1048576
  47.2 0.8 %copy.25 = bf16[128,2048]{1,0:T(8,128)(2,1)} copy(bf16[128,2048]{1,0:T(8,128)(2,1)S(1)} %get-tuple-element.31) | data formatting | bytes 1048576
  48.0 0.8 %copy.26 = bf16[128,2048]{1,0:T(8,128)(2,1)} copy(bf16[128,2048]{1,0:T(8,128)(2,1)S(1)} %get-tuple-element.32) | data formatting | bytes 1048576
  48.8 0.8 %copy.27 = bf16[128,2048]{1,0:T(8,128)(2,1)} copy(bf16[128,2048]{1,0:T(8,128)(2,1)S(1)} %get-tuple-element.33) | data formatting | bytes 1048576
  49.6 0.8 %copy.28 = bf16[128,2048]{1,0:T(8,128)(2,1)} copy(bf16[128,2048]{1,0:T(8,128)(2,1)S(1)} %get-tuple-element.34) | data formatting | bytes 1048576
  50.4 0.6 %copy.29 = f32[7,2048]{1,0:T(8,128)} copy(f32[7,2048]{1,0:T(8,128)S(1)} %bitcast.3) | data formatting | bytes 114688
Async XLA Ops:
  1.3 1.0 %copy-start = (bf16[128,2048]{1,0:T(8,128)(2,1)S(1)}, bf16[128,2048]{1,0:T(8,128)(2,1)}, u32[]{:S(2)}) copy-start(bf16[128,2048]{1,0:T(8,128)(2,1)} %vp.1) | copy-start | bytes 1572868
  2.4 1.0 %copy-start.1 = (bf16[128,2048]{1,0:T(8,128)(2,1)S(1)}, bf16[128,2048]{1,0:T(8,128)(2,1)}, u32[]{:S(2)}) copy-start(bf16[128,2048]{1,0:T(8,128)(2,1)} %ks.1) | copy-start | bytes 1572868
  3.4 1.0 %copy-start.2 = (bf16[128,2048]{1,0:T(8,128)(2,1)S(1)}, bf16[128,2048]{1,0:T(8,128)(2,1)}, u32[]{:S(2)}) copy-start(bf16[128,2048]{1,0:T(8,128)(2,1)} %qs.1) | copy-start | bytes 1572868
  4.4 1.0 %copy-start.3 = (bf16[128,2048]{1,0:T(8,128)(2,1)S(1)}, bf16[128,2048]{1,0:T(8,128)(2,1)}, u32[]{:S(2)}) copy-start(bf16[128,2048]{1,0:T(8,128)(2,1)} %km.1) | copy-start | bytes 1572868
  5.5 1.0 %copy-start.4 = (bf16[128,2048]{1,0:T(8,128)(2,1)S(1)}, bf16[128,2048]{1,0:T(8,128)(2,1)}, u32[]{:S(2)}) copy-start(bf16[128,2048]{1,0:T(8,128)(2,1)} %qm.1) | copy-start | bytes 1572868
  6.5 0.8 %copy-start.5 = (bf16[7,2048]{1,0:T(8,128)(2,1)S(1)}, bf16[7,2048]{1,0:T(8,128)(2,1)}, u32[]{:S(2)}) copy-start(bf16[7,2048]{1,0:T(8,128)(2,1)} %fse.1) | copy-start | bytes 86020

commit v2 on v1

--- a/solution.py
+++ b/solution.py
@@ -33,13 +33,16 @@
     near = np.concatenate([fh[:, :rows], fl[:, :rows]], axis=1)
     far = np.concatenate([fh[:, rows:], fl[:, rows:]], axis=1)
     bh, bl = split(bwd)
-    return np.stack([fh, fl, near, far, bh, bl])
+    first = np.concatenate([bh[:rows], bl[:rows]], axis=0)
+    last = np.concatenate([bh[rows:], bl[rows:]], axis=0)
+    return np.stack([fh, fl, near, far, first, last])
 
 
 def body(
-    n, ntp, fused, eps,
-    vp, ks, qs, km, qm, og, gain, fse, fmr, mats,
+    n, ntp, fused,
+    vp_h, ks_h, qs_h, km_h, qm_h, og_h, gain_h, fse_h, fmr_h, mats_h,
     o_val, o_qse, o_kse, o_qmr, o_kmr, o_small, o_fmr,
+    vp, ks, qs, km, qm, og, gain_in, gain, fse, fmr, mats, in_sem,
     win_se, g2, wsend, wh, conv, fs, os_, gp, win_gs, acc, row_send, row_recv, inv_send, invl_row, inv2, invl2, k2,
     pfb, own, rc, sx, rx, ag_own, ag_x, ag_c, sm, rs_s, ag_s,
     tail_sem, gh_s, gh_r, wh_s, wh_r, row_s, row_r, inv_sem, gs_sem,
@@ -69,6 +72,16 @@
     def wide(ref):
         return jnp.concatenate([ref[...]] * (CW // 128), axis=1)
 
+    fetch = [
+        pltpu.make_async_copy(src, dst, in_sem.at[i])
+        for i, (src, dst) in enumerate(
+            [(og_h, og), (qm_h, qm), (ks_h, ks), (vp_h, vp), (qs_h, qs), (fse_h, fse), (gain_h, gain_in), (km_h, km),
+             (mats_h, mats), (fmr_h, fmr)]
+        )
+    ]
+    for copy in fetch:
+        copy.start()
+
     bar = pltpu.get_barrier_semaphore()
     ctx_peers = [(me + d) % n for d in range(1, n)] if fused else [left, right]
     for p in ctx_peers:
@@ -87,6 +100,9 @@
         g2[pl.ds(rows, rows), :] = jnp.zeros((rows, chans), BF16)
         win_gs[pl.ds(rows, 8), :] = jnp.zeros((8, chans), F32)
 
+    for copy in fetch[:4]:
+        copy.wait()
+
     @pl.loop(0, nc)
     def _(c):
         ch = lanes(c)
@@ -115,6 +131,9 @@
             g_piece(h).start()
         tail.wait_recv()
 
+    for copy in fetch[4:8]:
+        copy.wait()
+    gain[...] = gain_in[...].astype(F32).reshape(1, chans)
     acc[...] = jnp.zeros_like(acc)
 
     def fold(x):
@@ -124,7 +143,8 @@
         return s
 
     @pl.loop(0, PIECES)
-    def _(h):
+    def _(step):
+        h = (right // 2 + 1 + step) % PIECES
         for i in range(per):
             ch = lanes(h * per + i)
             f = fse[:, ch].astype(F32)
@@ -166,12 +186,12 @@
     def dot(a, b):
         return jnp.dot(a, b, preferred_element_type=F32)
 
-    def back(y, at):
-        hi = y.astype(BF16)
-        lo = (y - hi.astype(F32)).astype(BF16)
-        bh = mats[4, pl.ds(at, rows), :]
-        bl = mats[5, pl.ds(at, rows), :]
-        return dot(bh, hi) + (dot(bl, hi) + dot(bh, lo))
+    def back(re, im, which):
+        both = dot(mats[which], jnp.concatenate([re.astype(BF16), im.astype(BF16)], axis=0))
+        return both[:rows] + both[rows:]
+
+    for copy in fetch[8:]:
+        copy.wait()
 
     @pl.loop(0, nc)
     def _(c):
@@ -206,7 +226,7 @@
             g = os_[:, ch] + dot(mats[3], twice(g2[pl.ds(rows, rows), ch]))
             gr, gi = g[:rows], g[rows:]
             fr, fi = fs[pl.ds(0, rows), ch], fs[pl.ds(rows, rows), ch]
-            grad = back(jnp.concatenate([gr * fr + gi * fi, gi * fr - gr * fi], axis=0), 0)
+            grad = back(gr * fr + gi * fi, gi * fr - gr * fi, 4)
             gp[:, ch] = grad
             mixed = qs[:, ch].astype(F32) * conv[:, ch]
             normed = (mixed * wide(inv2) * gain[:, ch]).astype(BF16)
@@ -218,8 +238,6 @@
     @pl.when(has_l)
     def _():
         inv_copy.wait_recv()
-        for h in range(PIECES):
-            w_piece(h).wait_recv()
 
     invl2[...] = jnp.broadcast_to(invl_row[0:1], (128, 128)).T
 
@@ -235,8 +253,8 @@
         xr, xi = x[:rows], x[rows:]
         gr, gi = os_[pl.ds(0, rows), ch], os_[pl.ds(rows, rows), ch]
         fr, fi = fs[pl.ds(0, rows), ch], fs[pl.ds(rows, rows), ch]
-        part = -back(jnp.concatenate([gr * xr + gi * xi, gi * xr - gr * xi], axis=0), rows)
-        y = back(jnp.concatenate([xr * fr - xi * fi, xr * fi + xi * fr], axis=0), rows)
+        part = -back(gr * xr + gi * xi, gi * xr - gr * xi, 5)
+        y = back(xr * fr - xi * fi, xr * fi + xi * fr, 5)
         o_qmr[:, ch] = (og[:, ch].astype(F32) * y).astype(BF16)
         return part
 
@@ -263,21 +281,30 @@
             src = ag_own if d == 0 else ag_x.at[d - 1]
             return remote(src, ag_c.at[d], agc_s.at[d], agc_r.at[d], {"ctx": mate})
 
-        @pl.loop(0, chips)
-        def _(i):
-            pfb[i] = medium(2 * i + 1 - core).astype(BF16)
-            to_mate(i).start()
-
-        @pl.loop(0, chips)
-        def _(i):
-            own[i] = medium(2 * i + core)
-
-        for d in range(1, chips):
-            to = (chip + d) % chips
-            to_mate(to).wait_recv()
-            sx[d - 1] = (own[to] + rc[to].astype(F32)).astype(BF16)
-            to_chip(d).start()
+        @pl.loop(1, chips + 1)
+        def _(d):
+            c = (chip + d) % chips
+
+            @pl.when(has_l)
+            def _():
+                w_piece(c).wait_recv()
+
+            pfb[c] = medium(2 * c + 1 - core).astype(BF16)
+            to_mate(c).start()
+            part = medium(2 * c + core)
+            to_mate(c).wait_recv()
+            own[...] = part + rc[c].astype(F32)
+
+            @pl.when(d < chips)
+            def _():
+                sx[d - 1] = own[...].astype(BF16)
+                to_chip(d).start()
     else:
+
+        @pl.when(has_l)
+        def _():
+            for h in range(PIECES):
+                w_piece(h).wait_recv()
 
         @pl.loop(0, nc)
         def _(c):
@@ -324,8 +351,7 @@
         for d in range(1, n):
             small_to(d).start()
 
-        to_mate(chip).wait_recv()
-        total = own[chip] + rc[chip].astype(F32)
+        total = own[...]
         for d in range(1, chips):
             to_chip(d).wait_recv()
             total = total + rx[d - 1].astype(F32)
@@ -397,6 +423,28 @@
             w_piece(h).wait_send()
 
 
+def write_out(val, qse, kse, qmr, kmr, small, gf, *rest):
+    outs, (o_fse, o_fmr, o_gain, fse, fmr, gain, sem) = rest[:5], rest[5:]
+    copies = [pltpu.make_async_copy(a, b, sem.at[i]) for i, (a, b) in enumerate(zip((val, qse, kse, qmr, kmr), outs))]
+    for copy in copies:
+        copy.start()
+    taps = fse.shape[0]
+    part = fmr.shape[0] // 4
+    for i in range(4):
+        at = pl.ds(i * part, part)
+        fmr[at, :] = gf[at, :].astype(F32)
+        copies.append(pltpu.make_async_copy(fmr.at[at], o_fmr.at[at], sem.at[5 + i]))
+        copies[-1].start()
+    fse[...] = small[pl.ds(0, taps), :]
+    gain[...] = small[pl.ds(taps, 1), :]
+    copies.append(pltpu.make_async_copy(fse, o_fse, sem.at[9]))
+    copies.append(pltpu.make_async_copy(gain, o_gain, sem.at[10]))
+    copies[-2].start()
+    copies[-1].start()
+    for copy in copies:
+        copy.wait()
+
+
 def shards(n, ntp, vp, ks, qs, km, qm, og, norm_gain, fse, fmr):
     rows, chans = vp.shape
     taps = fse.shape[0]
@@ -408,7 +456,13 @@
     wide_out = jax.ShapeDtypeStruct((rows, chans), BF16)
     dma = pltpu.SemaphoreType.DMA
     vmem = pltpu.VMEM
-    scratch = [
+    scratch = [vmem((rows, chans), BF16) for _ in range(6)] + [
+        vmem((chans,), BF16),
+        vmem((1, chans), F32),
+        vmem((taps, chans), BF16),
+        vmem(fmr.shape, BF16),
+        vmem((6, 2 * rows, 2 * rows), BF16),
+        dma((10,)),
         vmem((rows + 8, chans), F32),
         vmem((2 * rows, chans), BF16),
         vmem((rows, chans), BF16),
@@ -427,7 +481,7 @@
         vmem((rows, 128), F32),
         vmem((rows, 128), F32),
         vmem((chips,) + blk, BF16),
-        vmem((chips,) + blk, F32),
+        vmem(blk, F32),
         vmem((chips,) + blk, BF16),
         vmem((chips - 1,) + blk, BF16),
         vmem((chips - 1,) + blk, BF16),
@@ -452,22 +506,38 @@
     ]
     spec = pl.BlockSpec(memory_space=pltpu.VMEM)
     mats = jnp.asarray(matrices(rows))
+    operands = (vp, ks, qs, km, qm, og, norm_gain, fse, fmr, mats)
     outs = pl.pallas_call(
-        functools.partial(body, n, ntp, fused, 1e-06),
+        functools.partial(body, n, ntp, fused),
         out_shape=[wide_out] * 5
         + [jax.ShapeDtypeStruct((taps + 1, chans), F32), jax.ShapeDtypeStruct((rows, chans), BF16 if fused else F32)],
-        in_specs=[spec] * 10,
+        in_specs=[pl.BlockSpec(memory_space=pltpu.HBM)] * 10,
         out_specs=[spec] * 7,
         scratch_shapes=scratch,
         compiler_params=pltpu.CompilerParams(
-            collective_id=0, has_side_effects=True, vmem_limit_bytes=48 * 1024 * 1024
+            collective_id=0, has_side_effects=True, vmem_limit_bytes=40 * 1024 * 1024
         ),
         name="hyena_backward",
-    )(vp, ks, qs, km, qm, og, norm_gain.astype(F32).reshape(1, chans), fse, fmr, mats)
-    o_val, o_qse, o_kse, o_qmr, o_kmr, small, gf = outs
+    )(*(pltpu.with_memory_space_constraint(x, pltpu.HBM) for x in operands))
     if not fused:
-        small, gf = lax.psum((small, gf), "ctx")
-    return o_val, o_qse, o_kse, o_qmr, o_kmr, small[:taps], gf.astype(F32), small[taps]
+        small, gf = lax.psum(outs[5:], "ctx")
+        outs = list(outs[:5]) + [small, gf]
+    hbm = pl.BlockSpec(memory_space=pltpu.HBM)
+    done = pl.pallas_call(
+        write_out,
+        out_shape=[wide_out] * 5
+        + [
+            jax.ShapeDtypeStruct((taps, chans), F32),
+            jax.ShapeDtypeStruct((rows, chans), F32),
+            jax.ShapeDtypeStruct((1, chans), F32),
+        ],
+        in_specs=[spec] * 7,
+        out_specs=[hbm] * 8,
+        scratch_shapes=[vmem((taps, chans), F32), vmem((rows, chans), F32), vmem((1, chans), F32), dma((11,))],
+        compiler_params=pltpu.CompilerParams(vmem_limit_bytes=12 * 1024 * 1024),
+        name="write_out",
+    )(*outs)
+    return tuple(done[:7]) + (done[7].reshape(chans),)
 
 
 def solution(mesh):

time: 51.5 us -> 39.8 us (0.77)
  local copies, waits for them, and re-layouts: 11.2 us -> 0 us
  other arithmetic: 1.76 us -> 0 us
  Pallas kernels: 37.4 us -> 39 us
    unnamed x18 -> x0, local copies, waits for them, and re-layouts: 10.6 us -> none
    pallas_call x1 -> x2, Pallas kernels: 37.4 us -> 39 us  [the longest x1 37.1 us: shards(): pl.pallas_call(functools.partial(body, n, ntp, fused), out_shape=[wide_ou...]
    convert_element_type x1 -> x0, other arithmetic: 1.07 us -> none  [shards(): gf.astype(F32)]
    reshape x1 -> x0, other arithmetic: 0.69 us -> none  [shards(): norm_gain.astype(F32).reshape(1, chans)]
    slice x1 -> x0, local copies, waits for them, and re-layouts: 0.61 us -> none  [shards(): small[taps]]
where the time goes in v2:
time: 39.8 us; the launch traced here: 39.7 us
  Pallas kernels  39 us (98%)
  between operations  0.64 us (2%)
    pallas_call x1, Pallas kernels, shards(): pl.pallas_call(functools.partial(body, n, ntp, fused), out_shape=[wide_ou...  37.1 us
    pallas_call x1, Pallas kernels, shards(): pl.pallas_call(write_out, out_shape=[wide_out] * 5 + [jax.ShapeDtypeStruc...  1.94 us

profile of v2, /device:TPU:0, one launch (start us, length us, event | category | flops | bytes accessed | tf_op | source)
XLA Modules:
  0.0 39.7 jit_solution(15589851301738083877)
XLA Ops:
  0.6 37.1 %hyena_backward.1 = (bf16[128,2048]{1,0:T(8,128)(2,1)S(1)}, bf16[128,2048]{1,0:T(8,128)(2,1)S(1)}, bf16[128,2048]{1,0:T(8,128)(2,1)S(1)}, bf16[128,2048]{1,0:T(8...) custom-call(bf16[128,2048]{1,0:T(8,128)(2,1)} %vp_h.1, ...), custom_call_target="tpu_custom_call" | custom-call | tf_op jit(solution)/shard_map/hyena_backward/pallas_call | solution.py:510
  37.8 1.9 %write_out.1 = (bf16[128,2048]{1,0:T(8,128)(2,1)}, bf16[128,2048]{1,0:T(8,128)(2,1)}, bf16[128,2048]{1,0:T(8,128)(2,1)}, bf16[128,2048]{1,0:T(8,128)(2,1)}, bf16...) custom-call(bf16[128,2048]{1,0:T(8,128)(2,1)S(1)} %get-tuple-element.23.val, ...), custom_call_target="tpu_custom_call" | custom-call | tf_op jit(solution)/shard_map/write_out/pallas_call | solution.py:526

commit v3 on v2

--- a/solution.py
+++ b/solution.py
@@ -43,7 +43,7 @@
     vp_h, ks_h, qs_h, km_h, qm_h, og_h, gain_h, fse_h, fmr_h, mats_h,
     o_val, o_qse, o_kse, o_qmr, o_kmr, o_small, o_fmr,
     vp, ks, qs, km, qm, og, gain_in, gain, fse, fmr, mats, in_sem,
-    win_se, g2, wsend, wh, conv, fs, os_, gp, win_gs, acc, row_send, row_recv, inv_send, invl_row, inv2, invl2, k2,
+    win_se, g2, wsend, wh, conv, fs, os_, xs, gp, win_gs, acc, row_send, row_recv, inv_send, invl_row, inv2, invl2, k2,
     pfb, own, rc, sx, rx, ag_own, ag_x, ag_c, sm, rs_s, ag_s,
     tail_sem, gh_s, gh_r, wh_s, wh_r, row_s, row_r, inv_sem, gs_sem,
     rc_s, rc_r, rx_s, rx_r, agx_s, agx_r, agc_s, agc_r, rss_s, rss_r, ags_s, ags_r,
@@ -55,6 +55,7 @@
     nc = chans // CW
     hc = chans // PIECES
     per = hc // CW
+    tiles = CW // 128
     has_l = me > 0
     has_r = me < n - 1
     left = (me + n - 1) % n
@@ -68,6 +69,9 @@
 
     def lanes(c):
         return pl.ds(pl.multiple_of(c * CW, CW), CW)
+
+    def tile(t):
+        return pl.ds(pl.multiple_of(t * 128, 128), 128)
 
     def wide(ref):
         return jnp.concatenate([ref[...]] * (CW // 128), axis=1)
@@ -91,14 +95,14 @@
 
     @pl.when(jnp.logical_not(has_l))
     def _():
-        win_se[pl.ds(0, 8), :] = jnp.zeros((8, chans), F32)
+        win_se[:, pl.ds(0, 8), :] = jnp.zeros((chans // 128, 8, 128), F32)
         wh[...] = jnp.zeros_like(wh)
         invl_row[...] = jnp.zeros_like(invl_row)
 
     @pl.when(jnp.logical_not(has_r))
     def _():
         g2[pl.ds(rows, rows), :] = jnp.zeros((rows, chans), BF16)
-        win_gs[pl.ds(rows, 8), :] = jnp.zeros((8, chans), F32)
+        win_gs[:, pl.ds(rows, 8), :] = jnp.zeros((chans // 128, 8, 128), F32)
 
     for copy in fetch[:4]:
         copy.wait()
@@ -106,12 +110,14 @@
     @pl.loop(0, nc)
     def _(c):
         ch = lanes(c)
-        win_se[pl.ds(8, rows), ch] = (ks[:, ch].astype(F32) * vp[:, ch].astype(F32)).astype(BF16).astype(F32)
         g2[pl.ds(0, rows), ch] = (og[:, ch].astype(F32) * qm[:, ch].astype(F32)).astype(BF16)
+        prod = (ks[:, ch].astype(F32) * vp[:, ch].astype(F32)).astype(BF16).astype(F32)
+        for i in range(tiles):
+            win_se[c * tiles + i, pl.ds(8, rows), :] = prod[:, i * 128 : (i + 1) * 128]
 
     pl.semaphore_wait(bar, len(ctx_peers) + ntp - 1)
 
-    tail = remote(win_se.at[pl.ds(rows, 8)], win_se.at[pl.ds(0, 8)], tail_sem.at[0], tail_sem.at[1], {"ctx": right})
+    tail = remote(win_se.at[:, pl.ds(rows, 8)], win_se.at[:, pl.ds(0, 8)], tail_sem.at[0], tail_sem.at[1], {"ctx": right})
 
     def g_piece(h):
         hl = pl.ds(pl.multiple_of(h * hc, hc), hc)
@@ -145,15 +151,16 @@
     @pl.loop(0, PIECES)
     def _(step):
         h = (right // 2 + 1 + step) % PIECES
-        for i in range(per):
-            ch = lanes(h * per + i)
+        for i in range(hc // 128):
+            t = h * (hc // 128) + i
+            ch = tile(t)
             f = fse[:, ch].astype(F32)
-            cs = win_se[pl.ds(8, rows), ch] * f[0:1]
+            cs = win_se[t, pl.ds(8, rows), :] * f[0:1]
             for j in range(1, taps):
-                cs = cs + win_se[pl.ds(8 - j, rows), ch] * f[j : j + 1]
+                cs = cs + win_se[t, pl.ds(8 - j, rows), :] * f[j : j + 1]
             conv[:, ch] = cs
             mixed = qs[:, ch].astype(F32) * cs
-            acc[...] += fold(mixed * mixed)
+            acc[...] += mixed * mixed
             wsend[:, ch] = (mixed * gain[:, ch] * km[:, ch].astype(F32)).astype(BF16)
 
         @pl.when(has_r)
@@ -193,11 +200,12 @@
     for copy in fetch[8:]:
         copy.wait()
 
-    @pl.loop(0, nc)
-    def _(c):
-        ch = lanes(c)
-        fs[:, ch] = dot(mats[2], twice(fmr[:, ch]))
-        os_[:, ch] = dot(mats[2], twice(g2[pl.ds(0, rows), ch]))
+    @pl.loop(0, PIECES)
+    def _(h):
+        for i in range(per):
+            ch = lanes(h * per + i)
+            fs[:, ch] = dot(mats[2], twice(fmr[:, ch]))
+            os_[:, ch] = dot(mats[2], twice(g2[pl.ds(0, rows), ch]))
 
     inv_row = lax.rsqrt(gather(0) / D + 1e-06)
     inv_send[...] = inv_row
@@ -251,12 +259,16 @@
         window = jnp.concatenate([halo, prod], axis=0)
         x = dot(mats[0], window) + dot(mats[1], window)
         xr, xi = x[:rows], x[rows:]
+        xs[:, ch] = x
         gr, gi = os_[pl.ds(0, rows), ch], os_[pl.ds(rows, rows), ch]
+        return -back(gr * xr + gi * xi, gi * xr - gr * xi, 5)
+
+    def medium_out(c):
+        ch = lanes(c)
+        xr, xi = xs[pl.ds(0, rows), ch], xs[pl.ds(rows, rows), ch]
         fr, fi = fs[pl.ds(0, rows), ch], fs[pl.ds(rows, rows), ch]
-        part = -back(gr * xr + gi * xi, gi * xr - gr * xi, 5)
         y = back(xr * fr - xi * fi, xr * fi + xi * fr, 5)
         o_qmr[:, ch] = (og[:, ch].astype(F32) * y).astype(BF16)
-        return part
 
     if fused:
         chips = n // 2
@@ -289,16 +301,18 @@
             def _():
                 w_piece(c).wait_recv()
 
-            pfb[c] = medium(2 * c + 1 - core).astype(BF16)
+            theirs = medium(2 * c + 1 - core)
+            ours = medium(2 * c + core)
+            pfb[c] = theirs.astype(BF16)
             to_mate(c).start()
-            part = medium(2 * c + core)
-            to_mate(c).wait_recv()
-            own[...] = part + rc[c].astype(F32)
-
-            @pl.when(d < chips)
+            own[c] = ours
+
+            @pl.when(d > 1)
             def _():
-                sx[d - 1] = own[...].astype(BF16)
-                to_chip(d).start()
+                before = (chip + d - 1) % chips
+                to_mate(before).wait_recv()
+                sx[d - 2] = (own[before] + rc[before].astype(F32)).astype(BF16)
+                to_chip(d - 1).start()
     else:
 
         @pl.when(has_l)
@@ -316,21 +330,23 @@
 
     @pl.loop(0, nc)
     def _(c):
-        ch = lanes(c)
-        cs = conv[:, ch]
-        q = qs[:, ch].astype(F32)
-        mixed = q * cs
-        inv_w = wide(inv2)
-        grad_normed = gp[:, ch] * km[:, ch].astype(F32)
-        grad_mixed = inv_w * (grad_normed * gain[:, ch]) - mixed * wide(k2)
-        o_qse[:, ch] = (grad_mixed * cs).astype(BF16)
-        gcs = (grad_mixed * q).astype(BF16).astype(F32)
-        win_gs[pl.ds(0, rows), ch] = gcs
-        for j in range(taps):
-            sm[c, pl.ds(j, 1), :] = jnp.sum(gcs * win_se[pl.ds(8 - j, rows), ch], axis=0, keepdims=True)
-        sm[c, pl.ds(taps, 1), :] = jnp.sum(grad_normed * mixed * inv_w, axis=0, keepdims=True)
-
-    head = remote(win_gs.at[pl.ds(0, 8)], win_gs.at[pl.ds(rows, 8)], gs_sem.at[0], gs_sem.at[1], {"ctx": left})
+        for i in range(tiles):
+            t = c * tiles + i
+            at = pl.ds(i * 128, 128)
+            ch = tile(t)
+            cs = conv[:, ch]
+            q = qs[:, ch].astype(F32)
+            mixed = q * cs
+            grad_normed = gp[:, ch] * km[:, ch].astype(F32)
+            grad_mixed = inv2[...] * (grad_normed * gain[:, ch]) - mixed * k2[...]
+            o_qse[:, ch] = (grad_mixed * cs).astype(BF16)
+            sm[c, pl.ds(taps, 1), at] = jnp.sum(grad_normed * mixed * inv2[...], axis=0, keepdims=True)
+            gcs = (grad_mixed * q).astype(BF16).astype(F32)
+            win_gs[t, pl.ds(0, rows), :] = gcs
+            for j in range(taps):
+                sm[c, pl.ds(j, 1), at] = jnp.sum(gcs * win_se[t, pl.ds(8 - j, rows), :], axis=0, keepdims=True)
+
+    head = remote(win_gs.at[:, pl.ds(0, 8)], win_gs.at[:, pl.ds(rows, 8)], gs_sem.at[0], gs_sem.at[1], {"ctx": left})
 
     @pl.when(has_l)
     def _():
@@ -351,7 +367,8 @@
         for d in range(1, n):
             small_to(d).start()
 
-        total = own[...]
+        to_mate(chip).wait_recv()
+        total = own[chip] + rc[chip].astype(F32)
         for d in range(1, chips):
             to_chip(d).wait_recv()
             total = total + rx[d - 1].astype(F32)
@@ -360,6 +377,12 @@
             all_chip(d).start()
         all_mate(0).start()
 
+    @pl.loop(0, PIECES // 2)
+    def _(h):
+        for i in range(per):
+            medium_out(h * per + i)
+
+    if fused:
         total_s = sm[me]
         for d in range(1, n):
             small_to(d).wait_recv()
@@ -368,24 +391,33 @@
         for d in range(1, n):
             small_all(d).start()
 
-    @pl.when(has_r)
-    def _():
-        head.wait_recv()
-
-    @pl.loop(0, nc)
-    def _(c):
-        ch = lanes(c)
-        f = fse[:, ch].astype(F32)
-        g = win_gs[pl.ds(0, rows), ch] * f[0:1]
-        for j in range(1, taps):
-            g = g + win_gs[pl.ds(j, rows), ch] * f[j : j + 1]
-        o_kse[:, ch] = (g * vp[:, ch].astype(F32)).astype(BF16)
-        o_val[:, ch] = (g * ks[:, ch].astype(F32)).astype(BF16)
+    @pl.loop(PIECES // 2, PIECES)
+    def _(h):
+        for i in range(per):
+            medium_out(h * per + i)
 
     if fused:
         for d in range(1, chips):
             all_chip(d).wait_recv()
             all_mate(d).start()
+
+    @pl.when(has_r)
+    def _():
+        head.wait_recv()
+
+    @pl.loop(0, nc)
+    def _(c):
+        for i in range(tiles):
+            t = c * tiles + i
+            ch = tile(t)
+            f = fse[:, ch].astype(F32)
+            g = win_gs[t, pl.ds(0, rows), :] * f[0:1]
+            for j in range(1, taps):
+                g = g + win_gs[t, pl.ds(j, rows), :] * f[j : j + 1]
+            o_kse[:, ch] = (g * vp[:, ch].astype(F32)).astype(BF16)
+            o_val[:, ch] = (g * ks[:, ch].astype(F32)).astype(BF16)
+
+    if fused:
         o_fmr[:, lanes(me)] = ag_own[...]
         for d in range(1, chips):
             o_fmr[:, lanes(((chip + chips - d) % chips) * 2 + core)] = ag_x[d - 1]
@@ -463,15 +495,16 @@
         vmem(fmr.shape, BF16),
         vmem((6, 2 * rows, 2 * rows), BF16),
         dma((10,)),
-        vmem((rows + 8, chans), F32),
+        vmem((chans // 128, rows + 8, 128), F32),
         vmem((2 * rows, chans), BF16),
         vmem((rows, chans), BF16),
         vmem((rows, chans), BF16),
         vmem((rows, chans), F32),
         vmem((2 * rows, chans), F32),
         vmem((2 * rows, chans), F32),
+        vmem((2 * rows, chans), F32),
         vmem((rows, chans), F32),
-        vmem((rows + 8, chans), F32),
+        vmem((chans // 128, rows + 8, 128), F32),
         vmem((rows, 128), F32),
         vmem((2, 8, 128), F32),
         vmem((2, ntp - 1, 8, 128), F32),
@@ -481,7 +514,7 @@
         vmem((rows, 128), F32),
         vmem((rows, 128), F32),
         vmem((chips,) + blk, BF16),
-        vmem(blk, F32),
+        vmem((chips,) + blk, F32),
         vmem((chips,) + blk, BF16),
         vmem((chips - 1,) + blk, BF16),
         vmem((chips - 1,) + blk, BF16),

time: 39.8 us -> 36.7 us (0.922)
  Pallas kernels: 39 us -> 35.9 us
    pallas_call x1, Pallas kernels: 37.1 us -> 34 us  [shards(): pl.pallas_call(functools.partial(body, n, ntp, fused), out_shape=[wide_ou...]
where the time goes in v3:
time: 36.7 us; the launch traced here: 36.5 us
  Pallas kernels  35.9 us (98%)
  between operations  0.64 us (2%)
    pallas_call x1, Pallas kernels, shards(): pl.pallas_call(functools.partial(body, n, ntp, fused), out_shape=[wide_ou...  34 us
    pallas_call x1, Pallas kernels, shards(): pl.pallas_call(write_out, out_shape=[wide_out] * 5 + [jax.ShapeDtypeStruc...  1.94 us

profile of v3, /device:TPU:0, one launch (start us, length us, event | category | flops | bytes accessed | tf_op | source)
XLA Modules:
  0.0 36.5 jit_solution(15654517490341487840)
XLA Ops:
  0.6 34.0 %hyena_backward.1 = (bf16[128,2048]{1,0:T(8,128)(2,1)S(1)}, bf16[128,2048]{1,0:T(8,128)(2,1)S(1)}, bf16[128,2048]{1,0:T(8,128)(2,1)S(1)}, bf16[128,2048]{1,0:T(8...) custom-call(bf16[128,2048]{1,0:T(8,128)(2,1)} %vp_h.1, ...), custom_call_target="tpu_custom_call" | custom-call | tf_op jit(solution)/shard_map/hyena_backward/pallas_call | solution.py:543
  34.6 1.9 %write_out.1 = (bf16[128,2048]{1,0:T(8,128)(2,1)}, bf16[128,2048]{1,0:T(8,128)(2,1)}, bf16[128,2048]{1,0:T(8,128)(2,1)}, bf16[128,2048]{1,0:T(8,128)(2,1)}, bf16...) custom-call(bf16[128,2048]{1,0:T(8,128)(2,1)S(1)} %get-tuple-element.23.val, ...), custom_call_target="tpu_custom_call" | custom-call | tf_op jit(solution)/shard_map/write_out/pallas_call | solution.py:559

commit v4 on v3

--- a/solution.py
+++ b/solution.py
@@ -79,8 +79,8 @@
     fetch = [
         pltpu.make_async_copy(src, dst, in_sem.at[i])
         for i, (src, dst) in enumerate(
-            [(og_h, og), (qm_h, qm), (ks_h, ks), (vp_h, vp), (qs_h, qs), (fse_h, fse), (gain_h, gain_in), (km_h, km),
-             (mats_h, mats), (fmr_h, fmr)]
+            [(ks_h, ks), (vp_h, vp), (og_h, og), (qm_h, qm), (mats_h, mats), (fmr_h, fmr), (qs_h, qs), (fse_h, fse),
+             (gain_h, gain_in), (km_h, km)]
         )
     ]
     for copy in fetch:
@@ -104,13 +104,12 @@
         g2[pl.ds(rows, rows), :] = jnp.zeros((rows, chans), BF16)
         win_gs[:, pl.ds(rows, 8), :] = jnp.zeros((chans // 128, 8, 128), F32)
 
-    for copy in fetch[:4]:
+    for copy in fetch[:2]:
         copy.wait()
 
     @pl.loop(0, nc)
     def _(c):
         ch = lanes(c)
-        g2[pl.ds(0, rows), ch] = (og[:, ch].astype(F32) * qm[:, ch].astype(F32)).astype(BF16)
         prod = (ks[:, ch].astype(F32) * vp[:, ch].astype(F32)).astype(BF16).astype(F32)
         for i in range(tiles):
             win_se[c * tiles + i, pl.ds(8, rows), :] = prod[:, i * 128 : (i + 1) * 128]
@@ -131,13 +130,43 @@
     def _():
         tail.start()
 
+    for copy in fetch[2:4]:
+        copy.wait()
+
+    @pl.loop(0, PIECES)
+    def _(h):
+        for i in range(per):
+            ch = lanes(h * per + i)
+            g2[pl.ds(0, rows), ch] = (og[:, ch].astype(F32) * qm[:, ch].astype(F32)).astype(BF16)
+
+        @pl.when(has_l)
+        def _():
+            g_piece(h).start()
+
+    def twice(x):
+        return jnp.concatenate([x, x], axis=0)
+
+    def dot(a, b):
+        return jnp.dot(a, b, preferred_element_type=F32)
+
+    def back(re, im, which):
+        return dot(mats[which, pl.ds(0, rows), :], jnp.concatenate([re.astype(BF16), im.astype(BF16)], axis=0))
+
+    for copy in fetch[4:6]:
+        copy.wait()
+
+    @pl.loop(0, PIECES)
+    def _(h):
+        for i in range(per):
+            ch = lanes(h * per + i)
+            fs[:, ch] = dot(mats[2], twice(fmr[:, ch]))
+            os_[:, ch] = dot(mats[2], twice(g2[pl.ds(0, rows), ch]))
+
     @pl.when(has_l)
     def _():
-        for h in range(PIECES):
-            g_piece(h).start()
         tail.wait_recv()
 
-    for copy in fetch[4:8]:
+    for copy in fetch[6:]:
         copy.wait()
     gain[...] = gain_in[...].astype(F32).reshape(1, chans)
     acc[...] = jnp.zeros_like(acc)
@@ -187,40 +216,9 @@
 
     share(0)
 
-    def twice(x):
-        return jnp.concatenate([x, x], axis=0)
-
-    def dot(a, b):
-        return jnp.dot(a, b, preferred_element_type=F32)
-
-    def back(re, im, which):
-        both = dot(mats[which], jnp.concatenate([re.astype(BF16), im.astype(BF16)], axis=0))
-        return both[:rows] + both[rows:]
-
-    for copy in fetch[8:]:
-        copy.wait()
-
-    @pl.loop(0, PIECES)
-    def _(h):
-        for i in range(per):
-            ch = lanes(h * per + i)
-            fs[:, ch] = dot(mats[2], twice(fmr[:, ch]))
-            os_[:, ch] = dot(mats[2], twice(g2[pl.ds(0, rows), ch]))
-
-    inv_row = lax.rsqrt(gather(0) / D + 1e-06)
-    inv_send[...] = inv_row
-    inv_copy = remote(inv_send, invl_row, inv_sem.at[0], inv_sem.at[1], {"ctx": right})
-
-    @pl.when(has_r)
-    def _():
-        inv_copy.start()
-
-    inv2[...] = jnp.broadcast_to(inv_row[0:1], (128, 128)).T
-
     acc[...] = jnp.zeros_like(acc)
 
-    @pl.loop(0, PIECES)
-    def _(h):
+    def input_grad(h):
         @pl.when(has_l)
         def _():
             g_piece(h).wait_send()
@@ -237,9 +235,21 @@
             grad = back(gr * fr + gi * fi, gi * fr - gr * fi, 4)
             gp[:, ch] = grad
             mixed = qs[:, ch].astype(F32) * conv[:, ch]
-            normed = (mixed * wide(inv2) * gain[:, ch]).astype(BF16)
-            o_kmr[:, ch] = (grad * normed.astype(F32)).astype(BF16)
             acc[...] += fold(grad * km[:, ch].astype(F32) * gain[:, ch] * mixed)
+
+    pl.loop(0, PIECES // 2)(input_grad)
+
+    inv_row = lax.rsqrt(gather(0) / D + 1e-06)
+    inv_send[...] = inv_row
+    inv_copy = remote(inv_send, invl_row, inv_sem.at[0], inv_sem.at[1], {"ctx": right})
+
+    @pl.when(has_r)
+    def _():
+        inv_copy.start()
+
+    inv2[...] = jnp.broadcast_to(inv_row[0:1], (128, 128)).T
+
+    pl.loop(PIECES // 2, PIECES)(input_grad)
 
     share(1)
 
@@ -257,7 +267,8 @@
         prod = (kmf * normed.astype(F32)).astype(BF16)
         halo = (wh[:, ch].astype(F32) * wide(invl2)).astype(BF16)
         window = jnp.concatenate([halo, prod], axis=0)
-        x = dot(mats[0], window) + dot(mats[1], window)
+        o_kmr[:, ch] = (gp[:, ch] * normed.astype(F32)).astype(BF16)
+        x = dot(mats[0], window)
         xr, xi = x[:rows], x[rows:]
         xs[:, ch] = x
         gr, gi = os_[pl.ds(0, rows), ch], os_[pl.ds(rows, rows), ch]

time: 36.7 us -> 35.9 us (0.978)
  Pallas kernels: 35.9 us -> 35.2 us
    pallas_call x1, Pallas kernels: 34 us -> 33.2 us  [shards(): pl.pallas_call(functools.partial(body, n, ntp, fused), out_shape=[wide_ou...]
where the time goes in v4:
time: 35.9 us; the launch traced here: 35.8 us
  Pallas kernels  35.2 us (98%)
  between operations  0.64 us (2%)
    pallas_call x1, Pallas kernels, shards(): pl.pallas_call(functools.partial(body, n, ntp, fused), out_shape=[wide_ou...  33.2 us
    pallas_call x1, Pallas kernels, shards(): pl.pallas_call(write_out, out_shape=[wide_out] * 5 + [jax.ShapeDtypeStruc...  1.94 us

profile of v4, /device:TPU:0, one launch (start us, length us, event | category | flops | bytes accessed | tf_op | source)
XLA Modules:
  0.0 35.8 jit_solution(5625391558878344477)
XLA Ops:
  0.6 33.2 %hyena_backward.1 = (bf16[128,2048]{1,0:T(8,128)(2,1)S(1)}, bf16[128,2048]{1,0:T(8,128)(2,1)S(1)}, bf16[128,2048]{1,0:T(8,128)(2,1)S(1)}, bf16[128,2048]{1,0:T(8...) custom-call(bf16[128,2048]{1,0:T(8,128)(2,1)} %vp_h.1, ...), custom_call_target="tpu_custom_call" | custom-call | tf_op jit(solution)/shard_map/hyena_backward/pallas_call | solution.py:554
  33.9 1.9 %write_out.1 = (bf16[128,2048]{1,0:T(8,128)(2,1)}, bf16[128,2048]{1,0:T(8,128)(2,1)}, bf16[128,2048]{1,0:T(8,128)(2,1)}, bf16[128,2048]{1,0:T(8,128)(2,1)}, bf16...) custom-call(bf16[128,2048]{1,0:T(8,128)(2,1)S(1)} %get-tuple-element.23.val, ...), custom_call_target="tpu_custom_call" | custom-call | tf_op jit(solution)/shard_map/write_out/pallas_call | solution.py:570

commit v5 on v4

--- a/solution.py
+++ b/solution.py
@@ -31,11 +31,8 @@
     bwd = np.concatenate([np.cos(ang).T, -np.sin(ang).T], axis=1) / rows
     fh, fl = split(fwd)
     near = np.concatenate([fh[:, :rows], fl[:, :rows]], axis=1)
-    far = np.concatenate([fh[:, rows:], fl[:, rows:]], axis=1)
-    bh, bl = split(bwd)
-    first = np.concatenate([bh[:rows], bl[:rows]], axis=0)
-    last = np.concatenate([bh[rows:], bl[rows:]], axis=0)
-    return np.stack([fh, fl, near, far, first, last])
+    bh = bwd.astype(ml_dtypes.bfloat16)
+    return np.stack([fh, near, bh])
 
 
 def body(
@@ -43,9 +40,9 @@
     vp_h, ks_h, qs_h, km_h, qm_h, og_h, gain_h, fse_h, fmr_h, mats_h,
     o_val, o_qse, o_kse, o_qmr, o_kmr, o_small, o_fmr,
     vp, ks, qs, km, qm, og, gain_in, gain, fse, fmr, mats, in_sem,
-    win_se, g2, wsend, wh, conv, fs, os_, xs, gp, win_gs, acc, row_send, row_recv, inv_send, invl_row, inv2, invl2, k2,
+    win_se, g2, wsend, wh, conv, fs, gs, gp, win_gs, acc, row_send, row_recv, inv2, k2,
     pfb, own, rc, sx, rx, ag_own, ag_x, ag_c, sm, rs_s, ag_s,
-    tail_sem, gh_s, gh_r, wh_s, wh_r, row_s, row_r, inv_sem, gs_sem,
+    tail_sem, gh_s, gh_r, wh_s, wh_r, row_s, row_r, gs_sem,
     rc_s, rc_r, rx_s, rx_r, agx_s, agx_r, agc_s, agc_r, rss_s, rss_r, ags_s, ags_r,
 ):
     me = lax.axis_index("ctx")
@@ -97,7 +94,6 @@
     def _():
         win_se[:, pl.ds(0, 8), :] = jnp.zeros((chans // 128, 8, 128), F32)
         wh[...] = jnp.zeros_like(wh)
-        invl_row[...] = jnp.zeros_like(invl_row)
 
     @pl.when(jnp.logical_not(has_r))
     def _():
@@ -149,8 +145,8 @@
     def dot(a, b):
         return jnp.dot(a, b, preferred_element_type=F32)
 
-    def back(re, im, which):
-        return dot(mats[which, pl.ds(0, rows), :], jnp.concatenate([re.astype(BF16), im.astype(BF16)], axis=0))
+    def back(re, im, at):
+        return dot(mats[2, pl.ds(at, rows), :], jnp.concatenate([re.astype(BF16), im.astype(BF16)], axis=0))
 
     for copy in fetch[4:6]:
         copy.wait()
@@ -159,8 +155,7 @@
     def _(h):
         for i in range(per):
             ch = lanes(h * per + i)
-            fs[:, ch] = dot(mats[2], twice(fmr[:, ch]))
-            os_[:, ch] = dot(mats[2], twice(g2[pl.ds(0, rows), ch]))
+            fs[:, ch] = dot(mats[1], twice(fmr[:, ch]))
 
     @pl.when(has_l)
     def _():
@@ -178,8 +173,7 @@
         return s
 
     @pl.loop(0, PIECES)
-    def _(step):
-        h = (right // 2 + 1 + step) % PIECES
+    def _(h):
         for i in range(hc // 128):
             t = h * (hc // 128) + i
             ch = tile(t)
@@ -190,11 +184,6 @@
             conv[:, ch] = cs
             mixed = qs[:, ch].astype(F32) * cs
             acc[...] += mixed * mixed
-            wsend[:, ch] = (mixed * gain[:, ch] * km[:, ch].astype(F32)).astype(BF16)
-
-        @pl.when(has_r)
-        def _():
-            w_piece(h).start()
 
     def share(k):
         row_send[k] = jnp.broadcast_to(jnp.sum(acc[...].T, axis=0, keepdims=True), (8, 128))
@@ -229,56 +218,39 @@
 
         for i in range(per):
             ch = lanes(h * per + i)
-            g = os_[:, ch] + dot(mats[3], twice(g2[pl.ds(rows, rows), ch]))
+            g = dot(mats[0], g2[:, ch])
+            gs[:, ch] = g
             gr, gi = g[:rows], g[rows:]
             fr, fi = fs[pl.ds(0, rows), ch], fs[pl.ds(rows, rows), ch]
-            grad = back(gr * fr + gi * fi, gi * fr - gr * fi, 4)
+            grad = back(gr * fr + gi * fi, gi * fr - gr * fi, 0)
             gp[:, ch] = grad
             mixed = qs[:, ch].astype(F32) * conv[:, ch]
             acc[...] += fold(grad * km[:, ch].astype(F32) * gain[:, ch] * mixed)
 
-    pl.loop(0, PIECES // 2)(input_grad)
+    pl.loop(0, PIECES)(input_grad)
+    share(1)
 
     inv_row = lax.rsqrt(gather(0) / D + 1e-06)
-    inv_send[...] = inv_row
-    inv_copy = remote(inv_send, invl_row, inv_sem.at[0], inv_sem.at[1], {"ctx": right})
-
-    @pl.when(has_r)
-    def _():
-        inv_copy.start()
-
     inv2[...] = jnp.broadcast_to(inv_row[0:1], (128, 128)).T
-
-    pl.loop(PIECES // 2, PIECES)(input_grad)
-
-    share(1)
-
-    @pl.when(has_l)
-    def _():
-        inv_copy.wait_recv()
-
-    invl2[...] = jnp.broadcast_to(invl_row[0:1], (128, 128)).T
 
     def medium(c):
         ch = lanes(c)
-        kmf = km[:, ch].astype(F32)
         mixed = qs[:, ch].astype(F32) * conv[:, ch]
-        normed = (mixed * wide(inv2) * gain[:, ch]).astype(BF16)
-        prod = (kmf * normed.astype(F32)).astype(BF16)
-        halo = (wh[:, ch].astype(F32) * wide(invl2)).astype(BF16)
-        window = jnp.concatenate([halo, prod], axis=0)
-        o_kmr[:, ch] = (gp[:, ch] * normed.astype(F32)).astype(BF16)
-        x = dot(mats[0], window)
+        normed = (mixed * wide(inv2) * gain[:, ch]).astype(BF16).astype(F32)
+        prod = (km[:, ch].astype(F32) * normed).astype(BF16)
+        wsend[:, ch] = prod
+        o_kmr[:, ch] = (gp[:, ch] * normed).astype(BF16)
+        x = dot(mats[1], twice(prod))
         xr, xi = x[:rows], x[rows:]
-        xs[:, ch] = x
-        gr, gi = os_[pl.ds(0, rows), ch], os_[pl.ds(rows, rows), ch]
-        return -back(gr * xr + gi * xi, gi * xr - gr * xi, 5)
+        gr, gi = gs[pl.ds(0, rows), ch], gs[pl.ds(rows, rows), ch]
+        return back(gr * xr + gi * xi, gi * xr - gr * xi, 0)
 
     def medium_out(c):
         ch = lanes(c)
-        xr, xi = xs[pl.ds(0, rows), ch], xs[pl.ds(rows, rows), ch]
+        x = dot(mats[0], jnp.concatenate([wh[:, ch], wsend[:, ch]], axis=0))
+        xr, xi = x[:rows], x[rows:]
         fr, fi = fs[pl.ds(0, rows), ch], fs[pl.ds(rows, rows), ch]
-        y = back(xr * fr - xi * fi, xr * fi + xi * fr, 5)
+        y = back(xr * fr - xi * fi, xr * fi + xi * fr, rows)
         o_qmr[:, ch] = (og[:, ch].astype(F32) * y).astype(BF16)
 
     if fused:
@@ -308,15 +280,15 @@
         def _(d):
             c = (chip + d) % chips
 
-            @pl.when(has_l)
-            def _():
-                w_piece(c).wait_recv()
-
             theirs = medium(2 * c + 1 - core)
             ours = medium(2 * c + core)
             pfb[c] = theirs.astype(BF16)
             to_mate(c).start()
             own[c] = ours
+
+            @pl.when(has_r)
+            def _():
+                w_piece(c).start()
 
             @pl.when(d > 1)
             def _():
@@ -326,14 +298,15 @@
                 to_chip(d - 1).start()
     else:
 
-        @pl.when(has_l)
-        def _():
-            for h in range(PIECES):
-                w_piece(h).wait_recv()
-
-        @pl.loop(0, nc)
-        def _(c):
-            o_fmr[:, lanes(c)] = medium(c).astype(o_fmr.dtype)
+        @pl.loop(0, PIECES)
+        def _(h):
+            for i in range(per):
+                c = h * per + i
+                o_fmr[:, lanes(c)] = medium(c).astype(o_fmr.dtype)
+
+            @pl.when(has_r)
+            def _():
+                w_piece(h).start()
 
     dot_row = gather(1)
     inv = inv2[...]
@@ -388,10 +361,17 @@
             all_chip(d).start()
         all_mate(0).start()
 
-    @pl.loop(0, PIECES // 2)
-    def _(h):
+    def medium_piece(step):
+        h = (left // 2 + 1 + step) % PIECES
+
+        @pl.when(has_l)
+        def _():
+            w_piece(h).wait_recv()
+
         for i in range(per):
             medium_out(h * per + i)
+
+    pl.loop(0, PIECES // 2)(medium_piece)
 
     if fused:
         total_s = sm[me]
@@ -402,10 +382,7 @@
         for d in range(1, n):
             small_all(d).start()
 
-    @pl.loop(PIECES // 2, PIECES)
-    def _(h):
-        for i in range(per):
-            medium_out(h * per + i)
+    pl.loop(PIECES // 2, PIECES)(medium_piece)
 
     if fused:
         for d in range(1, chips):
@@ -461,7 +438,6 @@
     @pl.when(has_r)
     def _():
         tail.wait_send()
-        inv_copy.wait_send()
         for h in range(PIECES):
             w_piece(h).wait_send()
 
@@ -504,7 +480,7 @@
         vmem((1, chans), F32),
         vmem((taps, chans), BF16),
         vmem(fmr.shape, BF16),
-        vmem((6, 2 * rows, 2 * rows), BF16),
+        vmem((3, 2 * rows, 2 * rows), BF16),
         dma((10,)),
         vmem((chans // 128, rows + 8, 128), F32),
         vmem((2 * rows, chans), BF16),
@@ -513,15 +489,11 @@
         vmem((rows, chans), F32),
         vmem((2 * rows, chans), F32),
         vmem((2 * rows, chans), F32),
-        vmem((2 * rows, chans), F32),
         vmem((rows, chans), F32),
         vmem((chans // 128, rows + 8, 128), F32),
         vmem((rows, 128), F32),
         vmem((2, 8, 128), F32),
         vmem((2, ntp - 1, 8, 128), F32),
-        vmem((8, 128), F32),
-        vmem((8, 128), F32),
-        vmem((rows, 128), F32),
         vmem((rows, 128), F32),
         vmem((rows, 128), F32),
         vmem((chips,) + blk, BF16),
@@ -539,7 +511,6 @@
         dma((PIECES,)), dma((PIECES,)),
         dma((PIECES,)), dma((PIECES,)),
         dma((2, ntp - 1)), dma((2, ntp - 1)),
-        dma((2,)),
         dma((2,)),
         dma((chips,)), dma((chips,)),
         dma((chips - 1,)), dma((chips - 1,)),

time: 35.9 us -> 35.7 us (level)
  no operation moved by 1% of the time
where the time goes in v5:
time: 35.7 us; the launch traced here: 35.6 us
  Pallas kernels  34.9 us (98%)
  between operations  0.64 us (2%)
    pallas_call x1, Pallas kernels, shards(): pl.pallas_call(functools.partial(body, n, ntp, fused), out_shape=[wide_ou...  33 us
    pallas_call x1, Pallas kernels, shards(): pl.pallas_call(write_out, out_shape=[wide_out] * 5 + [jax.ShapeDtypeStruc...  1.94 us

profile of v5, /device:TPU:0, one launch (start us, length us, event | category | flops | bytes accessed | tf_op | source)
XLA Modules:
  0.0 35.6 jit_solution(18423330228399746017)
XLA Ops:
  0.6 33.0 %hyena_backward.1 = (bf16[128,2048]{1,0:T(8,128)(2,1)S(1)}, bf16[128,2048]{1,0:T(8,128)(2,1)S(1)}, bf16[128,2048]{1,0:T(8,128)(2,1)S(1)}, bf16[128,2048]{1,0:T(8...) custom-call(bf16[128,2048]{1,0:T(8,128)(2,1)} %vp_h.1, ...), custom_call_target="tpu_custom_call" | custom-call | tf_op jit(solution)/shard_map/hyena_backward/pallas_call | solution.py:525
  33.6 1.9 %write_out.1 = (bf16[128,2048]{1,0:T(8,128)(2,1)}, bf16[128,2048]{1,0:T(8,128)(2,1)}, bf16[128,2048]{1,0:T(8,128)(2,1)}, bf16[128,2048]{1,0:T(8,128)(2,1)}, bf16...) custom-call(bf16[128,2048]{1,0:T(8,128)(2,1)S(1)} %get-tuple-element.23.val, ...), custom_call_target="tpu_custom_call" | custom-call | tf_op jit(solution)/shard_map/write_out/pallas_call | solution.py:541

commit v6 on v5

--- a/solution.py
+++ b/solution.py
@@ -70,6 +70,10 @@
     def tile(t):
         return pl.ds(pl.multiple_of(t * 128, 128), 128)
 
+    def order(chip, d):
+        row, col = chip // 2, chip % 2
+        return (row + (4 - d) // 2 * (1 - 2 * row)) * 2 + col + d % 2 * (1 - 2 * col)
+
     def wide(ref):
         return jnp.concatenate([ref[...]] * (CW // 128), axis=1)
 
@@ -262,15 +266,22 @@
         def to_mate(i):
             return remote(pfb.at[i], rc.at[i], rc_s.at[i], rc_r.at[i], {"ctx": mate})
 
-        def to_chip(d):
-            return remote(
-                sx.at[d - 1], rx.at[d - 1], rx_s.at[d - 1], rx_r.at[d - 1], {"ctx": ((chip + d) % chips) * 2 + core}
-            )
-
-        def all_chip(d):
-            return remote(
-                ag_own, ag_x.at[d - 1], agx_s.at[d - 1], agx_r.at[d - 1], {"ctx": ((chip + d) % chips) * 2 + core}
-            )
+        cy, cx = chip // 2, chip % 2
+        over_y = ((1 - cy) * 2 + cx) * 2 + core
+        over_x = (cy * 2 + 1 - cx) * 2 + core
+
+        def to_y(k):
+            return remote(sx.at[k], rx.at[k], rx_s.at[k], rx_r.at[k], {"ctx": over_y})
+
+        def to_x():
+            return remote(sx.at[2], rx.at[2], rx_s.at[2], rx_r.at[2], {"ctx": over_x})
+
+        def all_x():
+            return remote(ag_own, ag_x.at[0], agx_s.at[0], agx_r.at[0], {"ctx": over_x})
+
+        def all_y(k):
+            src = ag_own if k == 0 else ag_x.at[0]
+            return remote(src, ag_x.at[1 + k], agx_s.at[1 + k], agx_r.at[1 + k], {"ctx": over_y})
 
         def all_mate(d):
             src = ag_own if d == 0 else ag_x.at[d - 1]
@@ -278,8 +289,7 @@
 
         @pl.loop(1, chips + 1)
         def _(d):
-            c = (chip + d) % chips
-
+            c = order(chip, d)
             theirs = medium(2 * c + 1 - core)
             ours = medium(2 * c + core)
             pfb[c] = theirs.astype(BF16)
@@ -290,12 +300,18 @@
             def _():
                 w_piece(c).start()
 
-            @pl.when(d > 1)
+            @pl.when((d > 1) & (d < chips))
             def _():
-                before = (chip + d - 1) % chips
+                before = order(chip, d - 1)
                 to_mate(before).wait_recv()
                 sx[d - 2] = (own[before] + rc[before].astype(F32)).astype(BF16)
-                to_chip(d - 1).start()
+                to_y(d - 2).start()
+
+        before = order(chip, 3)
+        to_mate(before).wait_recv()
+        to_y(0).wait_recv()
+        sx[2] = (own[before] + rc[before].astype(F32) + rx[0].astype(F32)).astype(BF16)
+        to_x().start()
     else:
 
         @pl.loop(0, PIECES)
@@ -353,16 +369,16 @@
 
         to_mate(chip).wait_recv()
         total = own[chip] + rc[chip].astype(F32)
-        for d in range(1, chips):
-            to_chip(d).wait_recv()
-            total = total + rx[d - 1].astype(F32)
+        to_y(1).wait_recv()
+        to_x().wait_recv()
+        total = total + rx[1].astype(F32) + rx[2].astype(F32)
         ag_own[...] = total.astype(BF16)
-        for d in range(1, chips):
-            all_chip(d).start()
+        all_x().start()
+        all_y(0).start()
         all_mate(0).start()
 
     def medium_piece(step):
-        h = (left // 2 + 1 + step) % PIECES
+        h = order((left // 2) % PIECES, step + 1)
 
         @pl.when(has_l)
         def _():
@@ -374,6 +390,9 @@
     pl.loop(0, PIECES // 2)(medium_piece)
 
     if fused:
+        all_x().wait_recv()
+        all_y(1).start()
+        all_mate(1).start()
         total_s = sm[me]
         for d in range(1, n):
             small_to(d).wait_recv()
@@ -385,9 +404,9 @@
     pl.loop(PIECES // 2, PIECES)(medium_piece)
 
     if fused:
-        for d in range(1, chips):
-            all_chip(d).wait_recv()
-            all_mate(d).start()
+        for k in range(2):
+            all_y(k).wait_recv()
+            all_mate(2 + k).start()
 
     @pl.when(has_r)
     def _():
@@ -407,21 +426,24 @@
 
     if fused:
         o_fmr[:, lanes(me)] = ag_own[...]
-        for d in range(1, chips):
-            o_fmr[:, lanes(((chip + chips - d) % chips) * 2 + core)] = ag_x[d - 1]
+        blocks = (chip, order(chip, 3), order(chip, 2), order(chip, 1))
+        for k in range(1, chips):
+            o_fmr[:, lanes(blocks[k] * 2 + core)] = ag_x[k - 1]
         o_small[:, lanes(me)] = ag_s[0]
         for d in range(1, n):
             small_all(d).wait_recv()
             o_small[:, lanes((me + n - d) % n)] = ag_s[d]
         for d in range(chips):
             all_mate(d).wait_recv()
-            o_fmr[:, lanes(((chip + chips - d) % chips) * 2 + 1 - core)] = ag_c[d]
+            o_fmr[:, lanes(blocks[d] * 2 + 1 - core)] = ag_c[d]
         for i in range(chips):
             to_mate(i).wait_send()
             all_mate(i).wait_send()
-        for d in range(1, chips):
-            to_chip(d).wait_send()
-            all_chip(d).wait_send()
+        for k in range(2):
+            to_y(k).wait_send()
+            all_y(k).wait_send()
+        to_x().wait_send()
+        all_x().wait_send()
         for d in range(1, n):
             small_to(d).wait_send()
             small_all(d).wait_send()
@@ -468,7 +490,7 @@
     rows, chans = vp.shape
     taps = fse.shape[0]
     nc = chans // CW
-    fused = n == nc and n % 2 == 0
+    fused = n == nc and n == 2 * PIECES
     chips = max(n // 2, 2) if fused else 2
     blk = (rows, CW)
     peers = n if fused else 2

time: 35.7 us -> 39.8 us (1.11)
  Pallas kernels: 34.9 us -> 39 us
    pallas_call x1, Pallas kernels: 33 us -> 37 us  [shards(): pl.pallas_call(functools.partial(body, n, ntp, fused), out_shape=[wide_ou...]
where the time goes in v6:
time: 39.8 us; the launch traced here: 39.6 us
  Pallas kernels  39 us (98%)
  between operations  0.64 us (2%)
    pallas_call x1, Pallas kernels, shards(): pl.pallas_call(functools.partial(body, n, ntp, fused), out_shape=[wide_ou...  37 us
    pallas_call x1, Pallas kernels, shards(): pl.pallas_call(write_out, out_shape=[wide_out] * 5 + [jax.ShapeDtypeStruc...  1.94 us

profile of v6, /device:TPU:0, one launch (start us, length us, event | category | flops | bytes accessed | tf_op | source)
XLA Modules:
  0.0 39.6 jit_solution(15648662925368178934)
XLA Ops:
  0.6 37.0 %hyena_backward.1 = (bf16[128,2048]{1,0:T(8,128)(2,1)S(1)}, bf16[128,2048]{1,0:T(8,128)(2,1)S(1)}, bf16[128,2048]{1,0:T(8,128)(2,1)S(1)}, bf16[128,2048]{1,0:T(8...) custom-call(bf16[128,2048]{1,0:T(8,128)(2,1)} %vp_h.1, ...), custom_call_target="tpu_custom_call" | custom-call | tf_op jit(solution)/shard_map/hyena_backward/pallas_call | solution.py:547
  37.7 1.9 %write_out.1 = (bf16[128,2048]{1,0:T(8,128)(2,1)}, bf16[128,2048]{1,0:T(8,128)(2,1)}, bf16[128,2048]{1,0:T(8,128)(2,1)}, bf16[128,2048]{1,0:T(8,128)(2,1)}, bf16...) custom-call(bf16[128,2048]{1,0:T(8,128)(2,1)S(1)} %get-tuple-element.23.val, ...), custom_call_target="tpu_custom_call" | custom-call | tf_op jit(solution)/shard_map/write_out/pallas_call | solution.py:563

commit v7 on v5

--- a/solution.py
+++ b/solution.py
@@ -40,9 +40,9 @@
     vp_h, ks_h, qs_h, km_h, qm_h, og_h, gain_h, fse_h, fmr_h, mats_h,
     o_val, o_qse, o_kse, o_qmr, o_kmr, o_small, o_fmr,
     vp, ks, qs, km, qm, og, gain_in, gain, fse, fmr, mats, in_sem,
-    win_se, g2, wsend, wh, conv, fs, gs, gp, win_gs, acc, row_send, row_recv, inv2, k2,
+    win_se, g2, wsend, wh, pr, conv, fs, gs, gp, win_gs, acc, row_send, row_recv, inv_send, invl_row, inv2, invl2, k2,
     pfb, own, rc, sx, rx, ag_own, ag_x, ag_c, sm, rs_s, ag_s,
-    tail_sem, gh_s, gh_r, wh_s, wh_r, row_s, row_r, gs_sem,
+    tail_sem, gh_s, gh_r, wh_s, wh_r, row_s, row_r, inv_sem, gs_sem,
     rc_s, rc_r, rx_s, rx_r, agx_s, agx_r, agc_s, agc_r, rss_s, rss_r, ags_s, ags_r,
 ):
     me = lax.axis_index("ctx")
@@ -94,6 +94,7 @@
     def _():
         win_se[:, pl.ds(0, 8), :] = jnp.zeros((chans // 128, 8, 128), F32)
         wh[...] = jnp.zeros_like(wh)
+        invl_row[...] = jnp.zeros_like(invl_row)
 
     @pl.when(jnp.logical_not(has_r))
     def _():
@@ -184,6 +185,11 @@
             conv[:, ch] = cs
             mixed = qs[:, ch].astype(F32) * cs
             acc[...] += mixed * mixed
+            wsend[:, ch] = (mixed * gain[:, ch] * km[:, ch].astype(F32)).astype(BF16)
+
+        @pl.when(has_r)
+        def _():
+            w_piece(h).start()
 
     def share(k):
         row_send[k] = jnp.broadcast_to(jnp.sum(acc[...].T, axis=0, keepdims=True), (8, 128))
@@ -231,6 +237,13 @@
     share(1)
 
     inv_row = lax.rsqrt(gather(0) / D + 1e-06)
+    inv_send[...] = inv_row
+    inv_copy = remote(inv_send, invl_row, inv_sem.at[0], inv_sem.at[1], {"ctx": right})
+
+    @pl.when(has_r)
+    def _():
+        inv_copy.start()
+
     inv2[...] = jnp.broadcast_to(inv_row[0:1], (128, 128)).T
 
     def medium(c):
@@ -238,7 +251,7 @@
         mixed = qs[:, ch].astype(F32) * conv[:, ch]
         normed = (mixed * wide(inv2) * gain[:, ch]).astype(BF16).astype(F32)
         prod = (km[:, ch].astype(F32) * normed).astype(BF16)
-        wsend[:, ch] = prod
+        pr[:, ch] = prod
         o_kmr[:, ch] = (gp[:, ch] * normed).astype(BF16)
         x = dot(mats[1], twice(prod))
         xr, xi = x[:rows], x[rows:]
@@ -247,7 +260,8 @@
 
     def medium_out(c):
         ch = lanes(c)
-        x = dot(mats[0], jnp.concatenate([wh[:, ch], wsend[:, ch]], axis=0))
+        halo = (wh[:, ch].astype(F32) * wide(invl2)).astype(BF16)
+        x = dot(mats[0], jnp.concatenate([halo, pr[:, ch]], axis=0))
         xr, xi = x[:rows], x[rows:]
         fr, fi = fs[pl.ds(0, rows), ch], fs[pl.ds(rows, rows), ch]
         y = back(xr * fr - xi * fi, xr * fi + xi * fr, rows)
@@ -285,10 +299,6 @@
             pfb[c] = theirs.astype(BF16)
             to_mate(c).start()
             own[c] = ours
-
-            @pl.when(has_r)
-            def _():
-                w_piece(c).start()
 
             @pl.when(d > 1)
             def _():
@@ -303,10 +313,6 @@
             for i in range(per):
                 c = h * per + i
                 o_fmr[:, lanes(c)] = medium(c).astype(o_fmr.dtype)
-
-            @pl.when(has_r)
-            def _():
-                w_piece(h).start()
 
     dot_row = gather(1)
     inv = inv2[...]
@@ -361,9 +367,13 @@
             all_chip(d).start()
         all_mate(0).start()
 
-    def medium_piece(step):
-        h = (left // 2 + 1 + step) % PIECES
-
+    @pl.when(has_l)
+    def _():
+        inv_copy.wait_recv()
+
+    invl2[...] = jnp.broadcast_to(invl_row[0:1], (128, 128)).T
+
+    def medium_piece(h):
         @pl.when(has_l)
         def _():
             w_piece(h).wait_recv()
@@ -438,6 +448,7 @@
     @pl.when(has_r)
     def _():
         tail.wait_send()
+        inv_copy.wait_send()
         for h in range(PIECES):
             w_piece(h).wait_send()
 
@@ -486,6 +497,7 @@
         vmem((2 * rows, chans), BF16),
         vmem((rows, chans), BF16),
         vmem((rows, chans), BF16),
+        vmem((rows, chans), BF16),
         vmem((rows, chans), F32),
         vmem((2 * rows, chans), F32),
         vmem((2 * rows, chans), F32),
@@ -494,6 +506,9 @@
         vmem((rows, 128), F32),
         vmem((2, 8, 128), F32),
         vmem((2, ntp - 1, 8, 128), F32),
+        vmem((8, 128), F32),
+        vmem((8, 128), F32),
+        vmem((rows, 128), F32),
         vmem((rows, 128), F32),
         vmem((rows, 128), F32),
         vmem((chips,) + blk, BF16),
@@ -511,6 +526,7 @@
         dma((PIECES,)), dma((PIECES,)),
         dma((PIECES,)), dma((PIECES,)),
         dma((2, ntp - 1)), dma((2, ntp - 1)),
+        dma((2,)),
         dma((2,)),
         dma((chips,)), dma((chips,)),
         dma((chips - 1,)), dma((chips - 1,)),

time: 35.7 us -> 36.2 us (1.014)
  Pallas kernels: 34.9 us -> 35.4 us
    pallas_call x1, Pallas kernels: 33 us -> 33.5 us  [shards(): pl.pallas_call(functools.partial(body, n, ntp, fused), out_shape=[wide_ou...]
where the time goes in v7:
time: 36.2 us; the launch traced here: 36 us
  Pallas kernels  35.4 us (98%)
  between operations  0.64 us (2%)
    pallas_call x1, Pallas kernels, shards(): pl.pallas_call(functools.partial(body, n, ntp, fused), out_shape=[wide_ou...  33.5 us
    pallas_call x1, Pallas kernels, shards(): pl.pallas_call(write_out, out_shape=[wide_out] * 5 + [jax.ShapeDtypeStruc...  1.94 us

profile of v7, /device:TPU:0, one launch (start us, length us, event | category | flops | bytes accessed | tf_op | source)
XLA Modules:
  0.0 36.0 jit_solution(11750629585043549824)
XLA Ops:
  0.6 33.5 %hyena_backward.1 = (bf16[128,2048]{1,0:T(8,128)(2,1)S(1)}, bf16[128,2048]{1,0:T(8,128)(2,1)S(1)}, bf16[128,2048]{1,0:T(8,128)(2,1)S(1)}, bf16[128,2048]{1,0:T(8...) custom-call(bf16[128,2048]{1,0:T(8,128)(2,1)} %vp_h.1, ...), custom_call_target="tpu_custom_call" | custom-call | tf_op jit(solution)/shard_map/hyena_backward/pallas_call | solution.py:541
  34.1 1.9 %write_out.1 = (bf16[128,2048]{1,0:T(8,128)(2,1)}, bf16[128,2048]{1,0:T(8,128)(2,1)}, bf16[128,2048]{1,0:T(8,128)(2,1)}, bf16[128,2048]{1,0:T(8,128)(2,1)}, bf16...) custom-call(bf16[128,2048]{1,0:T(8,128)(2,1)S(1)} %get-tuple-element.23.val, ...), custom_call_target="tpu_custom_call" | custom-call | tf_op jit(solution)/shard_map/write_out/pallas_call | solution.py:557
